TPU v7x, 512 devices: a whole 4x8x8 slice. The times are simulated.
512 devices in a mesh: row: 32 (over y_hi, z, core), col: 16 (over y_lo, x).
Axes of the slice: x: 4, y: 8 (y_hi: 2, y_lo: 4; y = y_hi * 4 + y_lo), z: 8, core: 2. Of those that a mesh axis runs over, the one named last changes fastest.
Arguments:
- features: bfloat16 [128, 96, 1536], P('row', 'col'), may hold values from -6 to 6
- kernel: float32 [49, 1536], replicated, may hold values from -0.875 to 0.875
- ln_gain: float32 [1536], replicated, may hold values from 0.25 to 1.75
- ln_bias: float32 [1536], replicated, may hold values from -3 to 3
- w_up: bfloat16 [1536, 4096], P(None, 'col'), may hold values from -0.15625 to 0.15625
- b_up: float32 [4096], P('col'), may hold values from -3 to 3
- w_down: bfloat16 [4096, 1536], P('col'), may hold values from -0.1875 to 0.1875
- layer_scale: float32 [1536], replicated, may hold values from 0.3 to 1.2
- text_embed: bfloat16 [6144, 1536], P(('row', 'col')), may hold values from -6 to 6
- slot_token: int32 [6144], P(('row', 'col')), may hold values from -1 to 95, as said below
- seq_grad: bfloat16 [6144, 1536], P(('row', 'col')), may hold values from -6 to 6
Outputs:
- seq_embed: bfloat16 [6144, 1536], P(('row', 'col'))
- grad_input: bfloat16 [128, 96, 1536], P('row', 'col')
- grad_kernel: float32 [49, 1536], replicated
- grad_up: bfloat16 [1536, 4096], P(None, 'col')
- grad_down: bfloat16 [4096, 1536], P('col')
Inputs may be any that keep to these rules, and one draw needn't show every extreme that they name: `slot_token`: -1 marks a text slot. In each band's slots every image token of the band appears exactly once, in row-major order of the band's tokens; half of the slots hold image tokens.
All inputs are finite; a program needn't handle non-finite values.
Results may differ from a plain program's by a relative error of at most 0.03.
Values may be sent and summed in bfloat16 or wider, within the bound.
A program may use at most 64 MiB of HBM per device.

v0:
```python
import jax
import jax.numpy as jnp
from jax import lax
from jax.sharding import PartitionSpec as P


def with_halo(cells, sides, width):
    for axis, dim in sides:
        count = lax.axis_size(axis)
        ends = count - 1
        head = lax.slice_in_dim(cells, 0, width, axis=dim)
        tail = lax.slice_in_dim(cells, cells.shape[dim] - width, cells.shape[dim], axis=dim)
        cells = jnp.concatenate(
            [
                lax.ppermute(tail, axis, [(i, (i + 1) % count) for i in range(ends)]),
                cells,
                lax.ppermute(head, axis, [((i + 1) % count, i) for i in range(ends)]),
            ],
            axis=dim,
        )
    return cells


def layer_norm(mixed, ln_gain, ln_bias):
    mean = jnp.mean(mixed, axis=-1, keepdims=True)
    centred = mixed - mean
    var = jnp.mean(centred * centred, axis=-1, keepdims=True)
    return centred * lax.rsqrt(var + 1e-06) * ln_gain + ln_bias


def gelu_tanh(value):
    return jax.nn.gelu(value, approximate=True)


def local(
    features,
    kernel,
    ln_gain,
    ln_bias,
    w_up,
    b_up,
    w_down,
    layer_scale,
    text_embed,
    slot_token,
    seq_grad,
):
    rows, cols, chans = features.shape
    half_rows, half_cols = (rows // 2, cols // 2)
    per_block = half_rows * half_cols
    pixels = rows * cols
    padded = with_halo(features, (("row", 0), ("col", 1)), 3)
    mixed = jnp.zeros((rows, cols, chans), jnp.float32)
    for tap in range(49):
        p, q = (tap // 7, tap % 7)
        mixed = mixed + padded[p : p + rows, q : q + cols].astype(jnp.float32) * kernel[tap]
    normed = layer_norm(mixed, ln_gain, ln_bias).astype(jnp.bfloat16)
    band_normed = lax.all_gather(normed.reshape(pixels, chans), "col", axis=0, tiled=True)
    pre = jnp.dot(band_normed, w_up, preferred_element_type=jnp.float32) + b_up
    act = gelu_tanh(pre).astype(jnp.bfloat16)
    piece = act
    branch = lax.psum_scatter(
        jnp.dot(piece, w_down, preferred_element_type=jnp.float32).astype(jnp.bfloat16),
        "col",
        scatter_dimension=0,
        tiled=True,
    ).astype(jnp.float32)
    summed = features.astype(jnp.float32) + layer_scale * branch.reshape(rows, cols, chans)
    tokens = summed.reshape(half_rows, 2, half_cols, 2, chans).mean(axis=(1, 3))
    tokens = tokens.astype(jnp.bfloat16).reshape(per_block, chans)
    band_tokens = lax.all_gather(tokens, "col", axis=0, tiled=True)
    band_count = band_tokens.shape[0]
    live = slot_token >= 0
    select = (slot_token[:, None] == jnp.arange(band_count, dtype=jnp.int32)[None, :]).astype(
        jnp.bfloat16
    )
    picked = jnp.dot(select, band_tokens, preferred_element_type=jnp.float32).astype(jnp.bfloat16)
    seq_embed = jnp.where(live[:, None], picked, text_embed)
    band_terms = lax.dot_general(
        select, seq_grad, (((0,), (0,)), ((), ())), preferred_element_type=jnp.float32
    )
    token_grad = lax.psum_scatter(
        band_terms.astype(jnp.bfloat16), "col", scatter_dimension=0, tiled=True
    ).astype(jnp.float32)
    token_grad = token_grad.reshape(half_rows, half_cols, chans)
    out_grad = jnp.repeat(jnp.repeat(token_grad / 4.0, 2, axis=0), 2, axis=1)
    branch_grad = (layer_scale * out_grad).astype(jnp.bfloat16).reshape(pixels, chans)
    piece = lax.all_gather(branch_grad, "col", axis=0, tiled=True)
    act_grad = jnp.einsum("pd,hd->ph", piece, w_down, preferred_element_type=jnp.float32)
    pre_grad = jax.vjp(gelu_tanh, pre)[1](act_grad)[0].astype(jnp.bfloat16)
    down_acc = jnp.einsum("ph,pd->hd", act, piece, preferred_element_type=jnp.float32)
    up_local = jnp.einsum("pd,ph->dh", band_normed, pre_grad, preferred_element_type=jnp.float32)
    piece = pre_grad
    normed_grad = lax.psum_scatter(
        jnp.einsum("ph,dh->pd", piece, w_up, preferred_element_type=jnp.float32).astype(
            jnp.bfloat16
        ),
        "col",
        scatter_dimension=0,
        tiled=True,
    ).astype(jnp.float32)
    norm_vjp = jax.vjp(lambda m: layer_norm(m, ln_gain, ln_bias), mixed)[1]
    mixed_grad = norm_vjp(normed_grad.reshape(rows, cols, chans))[0].astype(jnp.bfloat16)
    grad_padded = with_halo(mixed_grad, (("row", 0), ("col", 1)), 3)
    input_grad = out_grad
    mixed_wide = mixed_grad.astype(jnp.float32)
    kernel_rows = []
    for tap in range(49):
        p, q = (tap // 7, tap % 7)
        input_grad = (
            input_grad
            + grad_padded[6 - p : 6 - p + rows, 6 - q : 6 - q + cols].astype(jnp.float32)
            * kernel[tap]
        )
        kernel_rows.append(
            jnp.sum(
                padded[p : p + rows, q : q + cols].astype(jnp.float32) * mixed_wide, axis=(0, 1)
            )
        )
    kernel_local = jnp.stack(kernel_rows, axis=0)
    grad_kernel = lax.psum(kernel_local, ("row", "col"))
    grad_up, grad_down = (
        lax.psum(up_local.astype(jnp.bfloat16), "row").astype(jnp.float32),
        lax.psum(down_acc.astype(jnp.bfloat16), "row").astype(jnp.float32),
    )
    return (
        seq_embed,
        input_grad.astype(jnp.bfloat16),
        grad_kernel,
        grad_up.astype(jnp.bfloat16),
        grad_down.astype(jnp.bfloat16),
    )


def solution(mesh):
    placed = (
        P("row", "col", None),
        P(),
        P(),
        P(),
        P(None, "col"),
        P("col"),
        P("col", None),
        P(),
        P(("row", "col"), None),
        P(("row", "col")),
        P(("row", "col"), None),
    )
    return jax.shard_map(
        local,
        mesh=mesh,
        in_specs=placed,
        out_specs=(
            P(("row", "col"), None),
            P("row", "col", None),
            P(),
            P(None, "col"),
            P("col", None),
        ),
        check_vma=False,
    )
```

profile of v0, /device:TPU:1, one launch (start us, length us, event | category | flops | bytes accessed | tf_op | source)
XLA Modules:
  0.0 1055.8 jit_solution(8593405373701101507)
XLA Ops:
  8.5 40.3 %fusion = bf16[8,1536]{1,0:T(8,128)(2,1)S(1)} fusion(bf16[96,1536]{1,0:T(8,128)(2,1)S(1)} %convolution_convert_fusion.4), kind=kCustom, calls=%all-reduce-scatter | all-reduce-scatter fusion | flops 196609 | bytes 321536
  53.8 11.7 %collective-permute-start = (bf16[3,6,1536]{2,1,0:T(8,128)(2,1)S(1)}, bf16[3,6,1536]{2,1,0:T(8,128)(2,1)S(1)}, u32[]{:S(2)}, u32[]{:S(2)}) collective-permute-start(bf16[3,6,1536]{2,1,0:T(8,128)(2,1)S(1)} %copy.108), channel_id=1, source_target_pairs={{0,16},{16,32},{32,48},{48,64},{64,80},{80,96},{96,112},{112,128},... | collective-permute-start | bytes 165896 | tf_op jit(solution)/shard_map/ppermute | solution.py:15
  69.9 1.9 collective-permute-start.1
  73.5 2.1 collective-permute-done.1
  75.7 1.6 collective-permute-start.2
  79.4 3.7 collective-permute-done.3
  83.5 4.0 fusion.203
  88.7 65.1 %all-gather.6.cloned.1.call-done = bf16[384,1536]{1,0:T(8,128)(2,1)} async-done(((bf16[24,1536]{1,0:T(8,128)(2,1)}), bf16[384,1536]{1,0:T(8,128)(2,1)}) %all-gather.6.cloned.1.call-update) | async-done | bytes 1179664 | tf_op jit(solution)/shard_map/all_gather | solution.py:88
  153.8 2.5 fusion.209
  156.3 82.8 %all-gather.4.cloned.1.call-done = bf16[384,1536]{1,0:T(8,128)(2,1)} async-done(((bf16[24,1536]{1,0:T(8,128)(2,1)}), bf16[384,1536]{1,0:T(8,128)(2,1)}) %all-gather.4.cloned.1.call-update) | async-done | bytes 1179664 | tf_op jit(solution)/shard_map/all_gather | solution.py:58
  239.1 2.0 fusion.8
  245.9 2.9 convolution_convert_fusion.3
  250.3 79.0 %reduce-scatter.7.cloned.1.call-done = bf16[24,1536]{1,0:T(8,128)(2,1)} async-done(((bf16[384,1536]{1,0:T(8,128)(2,1)}), bf16[24,1536]{1,0:T(8,128)(2,1)}) %reduce-scatter.7.cloned.1.call-update) | async-done | bytes 73744 | tf_op jit(solution)/shard_map/reduce_scatter | solution.py:94
  331.2 14.9 %collective-permute-start.4 = (bf16[3,6,1536]{2,1,0:T(8,128)(2,1)S(1)}, bf16[3,6,1536]{2,1,0:T(8,128)(2,1)S(1)}, u32[]{:S(2)}, u32[]{:S(2)}) collective-permute-start(bf16[3,6,1536]{2,1,0:T(8,128)(2,1)S(1)} %get-tuple-element.142), channel_id=1, source_target_pairs={{0,16},{16,32},{32,48},{48,64},{64,80},{80,96},{96,112},{112,128},... | collective-permute-start | bytes 165896 | tf_op jit(solution)/shard_map/ppermute | solution.py:15
  346.1 1.9 collective-permute-start.5
  348.0 68.6 %reduce-scatter.5.cloned.1.call-done = bf16[24,1536]{1,0:T(8,128)(2,1)} async-done(((bf16[384,1536]{1,0:T(8,128)(2,1)}), bf16[24,1536]{1,0:T(8,128)(2,1)}) %reduce-scatter.5.cloned.1.call-update) | async-done | bytes 73744 | tf_op jit(solution)/shard_map/reduce_scatter | solution.py:62
  420.0 33.1 %all-gather = bf16[16,6,1536]{2,1,0:T(8,128)(2,1)S(1)} all-gather(bf16[1,6,1536]{2,1,0:T(8,128)(2,1)S(1)} %reshape.138), channel_id=1, replica_groups=mesh['row'=32,'col'=16] {'col'}, dimensions={0}, use_global_device_ids=true | all-gather | bytes 313344 | tf_op jit(solution)/shard_map/all_gather | solution.py:71
  453.9 4.8 stack.199
  460.6 4.0 collective-permute-start.7
  467.2 2.2 fusion.154
  470.1 304.2 %all-reduce.8.cloned.1.call-done = (bf16[1536,256]{1,0:T(8,128)(2,1)}, bf16[256,1536]{1,0:T(8,128)(2,1)}) async-done(((bf16[1536,256]{1,0:T(8,128)(2,1)}, bf16[256,1536]{1,0:T(8,128)(2,1)}), (bf16[1536,256]{1,0:T(8,128)(2,1)}, bf16[256,1536]{1,0:T(8,128)(2,1)})) %all-reduce.8.cloned.1.call-update) | async-done | bytes 1572880 | tf_op jit(solution)/shard_map/psum | solution.py:123
  774.3 269.9 %all-reduce.6.cloned.1.call-done = f32[49,1536]{1,0:T(8,128)} async-done(((f32[49,1536]{1,0:T(8,128)}), f32[49,1536]{1,0:T(8,128)}) %all-reduce.6.cloned.1.call-update) | async-done | bytes 301072 | tf_op jit(solution)/shard_map/psum | solution.py:121
  1044.3 1.7 copy.118
  1046.0 2.1 copy.119
  (318 shorter events, 31.7 us)
Async XLA Ops:
  7.2 231.9 %copy-start = (bf16[1536,256]{1,0:T(8,128)(2,1)S(1)}, bf16[1536,256]{1,0:T(8,128)(2,1)}, u32[]{:S(2)}) copy-start(bf16[1536,256]{1,0:T(8,128)(2,1)} %param.15) | copy-start | bytes 2359300
  7.2 59.8 %copy-start.5 = (f32[49,1536]{1,0:T(8,128)S(1)}, f32[49,1536]{1,0:T(8,128)}, u32[]{:S(2)}) copy-start(f32[49,1536]{1,0:T(8,128)} %param.12) | copy-start | bytes 903172
  7.2 146.6 %all-gather.6.cloned.1.call-start = ((), (), s32[]{:S(2)}) async-start(), calls=%async_computation.4 | async-start | bytes 1253376 | tf_op jit(solution)/shard_map/all_gather | solution.py:88
  48.8 23.0 %collective-permute-start.10 = (bf16[8,1536]{1,0:T(8,128)(2,1)S(1)}, bf16[8,1536]{1,0:T(8,128)(2,1)S(1)}, u32[]{:S(2)}, u32[]{:S(2)}) collective-permute-start(bf16[8,1536]{1,0:T(8,128)(2,1)S(1)} %fusion), channel_id=1, source_target_pairs={{0,3},{1,4},{2,5},{3,6},{4,7},{5,8},{6,9},{7,10},{8,11},{9,12},{10... | collective-permute-start | bytes 73736
  50.1 21.7 %collective-permute-start.8 = (bf16[8,1536]{1,0:T(8,128)(2,1)S(1)}, bf16[8,1536]{1,0:T(8,128)(2,1)S(1)}, u32[]{:S(2)}, u32[]{:S(2)}) collective-permute-start(bf16[8,1536]{1,0:T(8,128)(2,1)S(1)} %fusion), channel_id=1, source_target_pairs={{0,1},{1,2},{2,3},{3,4},{4,5},{5,6},{6,7},{7,8},{8,9},{9,10},{10,1... | collective-permute-start | bytes 73736
  51.4 20.5 %collective-permute-start.9 = (bf16[8,1536]{1,0:T(8,128)(2,1)S(1)}, bf16[8,1536]{1,0:T(8,128)(2,1)S(1)}, u32[]{:S(2)}, u32[]{:S(2)}) collective-permute-start(bf16[8,1536]{1,0:T(8,128)(2,1)S(1)} %fusion), channel_id=1, source_target_pairs={{0,2},{1,3},{2,4},{3,5},{4,6},{5,7},{6,8},{7,9},{8,10},{9,11},{10,... | collective-permute-start | bytes 73736
  53.8 19.6 %collective-permute-start = (bf16[3,6,1536]{2,1,0:T(8,128)(2,1)S(1)}, bf16[3,6,1536]{2,1,0:T(8,128)(2,1)S(1)}, u32[]{:S(2)}, u32[]{:S(2)}) collective-permute-start(bf16[3,6,1536]{2,1,0:T(8,128)(2,1)S(1)} %copy.108), channel_id=1, source_target_pairs={{0,16},{16,32},{32,48},{48,64},{64,80},{80,96},{96,112},{112,128},... | collective-permute-start | bytes 165896 | tf_op jit(solution)/shard_map/ppermute | solution.py:15
  65.5 4.4 collective-permute-start.11
  69.9 5.7 collective-permute-start.1
  73.3 165.7 %all-gather.4.cloned.1.call-start = ((), (), s32[]{:S(2)}) async-start(), calls=%async_computation.2 | async-start | bytes 1253376 | tf_op jit(solution)/shard_map/all_gather | solution.py:58
  75.7 3.7 collective-permute-start.2
  77.3 5.9 collective-permute-start.3
  83.5 70.3 %copy-start.1 = (bf16[256,1536]{1,0:T(8,128)(2,1)S(1)}, bf16[256,1536]{1,0:T(8,128)(2,1)}, u32[]{:S(2)}) copy-start(bf16[256,1536]{1,0:T(8,128)(2,1)} %param.17) | copy-start | bytes 2359300
  88.6 150.4 %copy-start.92 = (f32[256]{0:T(256)S(1)}, f32[256]{0:T(256)}, u32[]{:S(2)}) copy-start(f32[256]{0:T(256)} %param.16) | copy-start | bytes 3076
  88.6 240.7 %reduce-scatter.7.cloned.1.call-start = ((), (), s32[]{:S(2)}) async-start(), calls=%async_computation.5 | async-start | bytes 1253376 | tf_op jit(solution)/shard_map/reduce_scatter | solution.py:94
  243.3 173.3 %reduce-scatter.5.cloned.1.call-start = ((), (), s32[]{:S(2)}) async-start(), calls=%async_computation.3 | async-start | bytes 1253376 | tf_op jit(solution)/shard_map/reduce_scatter | solution.py:62
  245.0 529.4 %all-reduce.8.cloned.1.call-start = ((), (), s32[]{:S(2)}) async-start(), calls=%async_computation.7 | async-start | bytes 3145728 | tf_op jit(solution)/shard_map/psum | solution.py:123
  250.3 794.0 %all-reduce.6.cloned.1.call-start = ((), (), s32[]{:S(2)}) async-start(), calls=%async_computation.6 | async-start | bytes 688128 | tf_op jit(solution)/shard_map/psum | solution.py:121
  330.2 87.4 %copy-start.89 = (f32[1536]{0:T(1024)S(1)}, f32[1536]{0:T(1024)}, u32[]{:S(2)}) copy-start(f32[1536]{0:T(1024)} %param.18) | copy-start | bytes 18436
  331.2 127.5 %collective-permute-start.4 = (bf16[3,6,1536]{2,1,0:T(8,128)(2,1)S(1)}, bf16[3,6,1536]{2,1,0:T(8,128)(2,1)S(1)}, u32[]{:S(2)}, u32[]{:S(2)}) collective-permute-start(bf16[3,6,1536]{2,1,0:T(8,128)(2,1)S(1)} %get-tuple-element.142), channel_id=1, source_target_pairs={{0,16},{16,32},{32,48},{48,64},{64,80},{80,96},{96,112},{112,128},... | collective-permute-start | bytes 165896 | tf_op jit(solution)/shard_map/ppermute | solution.py:15
  346.1 112.6 %collective-permute-start.5 = (bf16[3,6,1536]{2,1,0:T(8,128)(2,1)S(1)}, bf16[3,6,1536]{2,1,0:T(8,128)(2,1)S(1)}, u32[]{:S(2)}, u32[]{:S(2)}) collective-permute-start(bf16[3,6,1536]{2,1,0:T(8,128)(2,1)S(1)} %get-tuple-element.141), channel_id=1, source_target_pairs={{16,0},{32,16},{48,32},{64,48},{80,64},{96,80},{112,96},{128,112},... | collective-permute-start | bytes 165896 | tf_op jit(solution)/shard_map/ppermute | solution.py:17
  459.3 6.2 collective-permute-start.6
  460.6 5.8 collective-permute-start.7
  774.3 273.7 %copy-start.4 = (bf16[256,1536]{1,0:T(8,128)(2,1)S(1)}, bf16[256,1536]{1,0:T(8,128)(2,1)}, u32[]{:S(2)}) copy-start(bf16[256,1536]{1,0:T(8,128)(2,1)} %get-tuple-element.158) | copy-start | bytes 2359300
  (87 other events, 956.7 us)
Sparse Core Ops, SparseCore 0:
  73.5 80.2 all-gather.5
  156.4 82.5 all-gather.3
  243.4 85.7 reduce-scatter.6
  332.0 84.6 reduce-scatter.4
  420.0 354.2 all-reduce.7
  780.5 263.7 all-reduce.5
where the time goes:
time: 1060 us
  waiting for transfers between devices  877 us (83%)
  blocking collectives  73.4 us (7%)
  starting transfers between devices  44.2 us (4%)
  local copies, waits for them, and re-layouts  19.8 us (2%)
  between operations  16.9 us (2%)
  matrix products  14.1 us (1%)
  other arithmetic  10.8 us (1%)
    psum x1, waiting for transfers between devices, local(): lax.psum(up_local.astype(jnp.bfloat16), 'row').astype(jnp.float32)  304 us
    psum x1, waiting for transfers between devices, local(): grad_kernel = lax.psum(kernel_local, ('row', 'col'))  270 us
    all_gather x1, waiting for transfers between devices, local(): lax.all_gather(normed.reshape(pixels, chans), 'col', axis=0, tiled=True)  82.8 us
    reduce_scatter x1, waiting for transfers between devices, local(): lax.psum_scatter(jnp.einsum('ph,dh->pd', piece, w_up, preferred_element_t...  79 us
    reduce_scatter x1, waiting for transfers between devices, local(): lax.psum_scatter(jnp.dot(piece, w_down, preferred_element_type=jnp.float3...  68.6 us
    all_gather x1, waiting for transfers between devices, local(): piece = lax.all_gather(branch_grad, 'col', axis=0, tiled=True)  65.1 us
    unnamed x1, blocking collectives  40.3 us
    all_gather x1, blocking collectives, local(): band_tokens = lax.all_gather(tokens, 'col', axis=0, tiled=True)  33.1 us
  transfers between devices with their start and end apart: 18, of which 9 were waited for; matrix products, arithmetic and copies ran while one was open for 3% of the time, Pallas kernels for 0%

commit v1 on v0

v1 whole, which is shorter than its diff:
```python
import functools

import jax
import jax.numpy as jnp
import numpy as np
from jax import lax
from jax.experimental import pallas as pl
from jax.experimental.pallas import tpu as pltpu
from jax.sharding import PartitionSpec as P

F32, BF16 = jnp.float32, jnp.bfloat16
D, LANE, SUB = 1536, 128, 12
ROWS, COLS, PIX, SLOTS, SLOT_PAD = 4, 6, 24, 12, 16
N_ROW, N_COL = 32, 16
NX, NY = 4, 4
NZ, NC = 8, 2
HID = 256
DIRS = [(a, b) for a in (-1, 0, 1) for b in (-1, 0, 1) if (a, b) != (0, 0)]
MESH = pl.DeviceIdType.MESH
VMEM_LIMIT = 48 * 1024 * 1024
SRC_ROW = {1: (1, 3), 0: (0, 4), -1: (0, 3)}
DST_ROW = {1: 0, 0: 3, -1: 7}
SRC_COL = {1: (3, 3), 0: (0, 6), -1: (0, 3)}
DST_COL = {1: 0, 0: 3, -1: 9}


def remote(src, dst, send, recv, where):
    return pltpu.make_async_remote_copy(
        src_ref=src, dst_ref=dst, send_sem=send, recv_sem=recv, device_id=where, device_id_type=MESH
    )


def greet(where):
    barrier = pltpu.get_barrier_semaphore()
    for device in where:
        pl.semaphore_signal(barrier, inc=1, device_id=device, device_id_type=MESH)
    pl.semaphore_wait(barrier, len(where))


def halo_copies(pad, row, col, send, recv):
    out = []
    for k, (a, b) in enumerate(DIRS):
        r0, nr = SRC_ROW[a]
        c0, nc = SRC_COL[b]
        where = (lax.rem(row + a + N_ROW, N_ROW), lax.rem(col + b + N_COL, N_COL))
        out.append(
            remote(
                pad.at[pl.ds(3 + r0, nr), pl.ds(3 + c0, nc)],
                pad.at[pl.ds(DST_ROW[a], nr), pl.ds(DST_COL[b], nc)],
                send.at[k],
                recv.at[k],
                where,
            )
        )
    return out


def widen(pad, wide, row, col):
    top = jnp.where(row == 0, 0.0, 1.0)
    bottom = jnp.where(row == N_ROW - 1, 0.0, 1.0)
    left = jnp.where(col == 0, 0.0, 1.0)
    right = jnp.where(col == N_COL - 1, 0.0, 1.0)
    for a in range(ROWS + 6):
        edge = top if a < 3 else bottom if a >= 7 else 1.0
        wide[a, pl.ds(0, 3)] = pad[a, pl.ds(0, 3)].astype(F32) * (edge * left)
        if a < 3 or a >= 7:
            wide[a, pl.ds(3, 6)] = pad[a, pl.ds(3, 6)].astype(F32) * edge
        else:
            wide[a, pl.ds(3, 6)] = pad[a, pl.ds(3, 6)].astype(F32)
        wide[a, pl.ds(9, 3)] = pad[a, pl.ds(9, 3)].astype(F32) * (edge * right)


def row_of_taps(wide, kern, i, flip):
    def step(p, acc):
        line = wide[i + (6 - p if flip else p)]
        for q in range(7):
            s = 6 - q if flip else q
            acc = acc + line[s : s + COLS] * kern[p * 7 + q]
        return acc

    return lax.fori_loop(0, 7, step, jnp.zeros((COLS, SUB, LANE), F32))


def forward_kernel(
    feat, kern, gain, bias, slots, normed, slots_all, mixed, pad,
    wide, flat, halo_s, halo_r, n_s, n_r, g_s, g_r,
):
    row, col = lax.axis_index("row"), lax.axis_index("col")
    y, x = col // NX, lax.rem(col, NX)
    peer = lambda dy, dx: lax.rem(y + dy + NY, NY) * NX + lax.rem(x + dx + NX, NX)
    wherey = [(row, peer(dy, 0)) for dy in range(1, NY)]
    wherex = [(row, peer(0, dx)) for dx in range(1, NX)]
    around = [
        (lax.rem(row + a + N_ROW, N_ROW), lax.rem(col + b + N_COL, N_COL)) for a, b in DIRS
    ]
    pad[pl.ds(3, ROWS), pl.ds(3, COLS)] = feat[...]
    slots_all[col] = slots[...]
    greet(around + wherey + wherex)
    halo = halo_copies(pad, row, col, halo_s, halo_r)
    for c in halo:
        c.start()

    def own(ref, send, recv):
        for dy in range(1, NY):
            yield remote(ref.at[col], ref.at[col], send.at[dy, 0], recv.at[dy, 0], wherey[dy - 1])
        for dx in range(1, NX):
            yield remote(ref.at[col], ref.at[col], send.at[0, dx], recv.at[0, dx], wherex[dx - 1])

    def passed(ref, send, recv, dy, dx):
        block = ref.at[peer(-dy, 0)]
        return remote(block, block, send.at[dy, dx], recv.at[dy, dx], wherex[dx - 1])

    def came(ref, send, recv, dy, dx):
        block = ref.at[peer(-dy, -dx)]
        return remote(block, block, send.at[dy, dx], recv.at[dy, dx], (row, peer(dy, dx)))

    for c in own(slots_all, g_s, g_r):
        c.start()
    for c in halo:
        c.wait_recv()
    widen(pad, wide, row, col)

    def line(i, _):
        acc = row_of_taps(wide, kern, i, False)
        for j in range(COLS):
            flat[pl.ds(pl.multiple_of((i * COLS + j) * 16, 16), SUB)] = acc[j]
        return 0

    lax.fori_loop(0, ROWS, line, 0)
    for g in range(SUB):
        mixed[:, pl.ds(g * LANE, LANE)] = flat[pl.ds(g, PIX, stride=16)]
    m = mixed[...]
    centred = m - jnp.mean(m, axis=-1, keepdims=True)
    var = jnp.mean(centred * centred, axis=-1, keepdims=True)
    normed[col] = (centred * lax.rsqrt(var + 1e-06) * gain[...] + bias[...]).astype(BF16)
    for c in own(normed, n_s, n_r):
        c.start()
    for ref, send, recv in ((slots_all, g_s, g_r), (normed, n_s, n_r)):
        for dy in range(1, NY):
            came(ref, send, recv, dy, 0).wait_recv()
            for dx in range(1, NX):
                passed(ref, send, recv, dy, dx).start()
    for ref, send, recv in ((slots_all, g_s, g_r), (normed, n_s, n_r)):
        for dx in range(1, NX):
            for dy in range(NY):
                came(ref, send, recv, dy, dx).wait_recv()
    for ref, send, recv in ((slots_all, g_s, g_r), (normed, n_s, n_r)):
        for c in own(ref, send, recv):
            c.wait_send()
        for dy in range(1, NY):
            for dx in range(1, NX):
                passed(ref, send, recv, dy, dx).wait_send()
    for c in halo:
        c.wait_send()


def forward(feat, kern, gain, bias, slots):
    vm = pl.BlockSpec(memory_space=pltpu.VMEM)
    dma = pltpu.SemaphoreType.DMA
    return pl.pallas_call(
        forward_kernel,
        out_shape=(
            jax.ShapeDtypeStruct((N_COL, PIX, D), BF16),
            jax.ShapeDtypeStruct((N_COL, SLOT_PAD, D), BF16),
            jax.ShapeDtypeStruct((PIX, D), F32),
            jax.ShapeDtypeStruct((ROWS + 6, COLS + 6, SUB, LANE), BF16),
        ),
        in_specs=[vm] * 5,
        out_specs=[vm] * 4,
        scratch_shapes=[
            pltpu.VMEM((ROWS + 6, COLS + 6, SUB, LANE), F32),
            pltpu.VMEM((PIX * 16, LANE), F32),
            dma((8,)), dma((8,)),
            dma((NY, NX)), dma((NY, NX)),
            dma((NY, NX)), dma((NY, NX)),
        ],
        compiler_params=pltpu.CompilerParams(
            collective_id=0, has_side_effects=True, vmem_limit_bytes=VMEM_LIMIT
        ),
    )(feat, kern, gain, bias, slots)


def backward_kernel(
    ng, part, up, down, mixed, gain, kern, pad, og, slot, text,
    seq, gin, gker, gup, gdown,
    ng_in, part_in, up0, down0, up1, down1, up2, down2, up_h, down_h, up_c, down_c,
    mgpad, wide, mwide, flat, ker, ker_in, ker_z, ker_q, ker_out,
    ng_s, ng_r, part_s, part_r, halo_s, halo_r, c_s, c_r, z_s, z_r, h_s, h_r,
    a_s, a_r, b_s, b_r, k1_s, k1_r, k2_s, k2_r, k3_s, k3_r, k4_s, k4_r,
):
    row, col = lax.axis_index("row"), lax.axis_index("col")
    core = lax.rem(row, NC)
    z = lax.rem(row // NC, NZ)
    yh = row // (NC * NZ)
    at = lambda yy, zz, cc: ((yy * NZ + zz) * NC + cc, col)
    colp = [(row, lax.rem(col + k, N_COL)) for k in range(1, N_COL)]
    colb = [lax.rem(col + k, N_COL) for k in range(1, N_COL)]
    colf = [lax.rem(col - k + N_COL, N_COL) for k in range(1, N_COL)]
    zb = [lax.rem(z + k, NZ) for k in range(1, NZ)]
    zf = [lax.rem(z - k + NZ, NZ) for k in range(1, NZ)]
    zp = [at(yh, k, core) for k in zb]
    twin = at(yh, z, 1 - core)
    far = at(1 - yh, z, core)
    diag = at(1 - yh, z, 1 - core)
    around = [
        (lax.rem(row + a + N_ROW, N_ROW), lax.rem(col + b + N_COL, N_COL)) for a, b in DIRS
    ]
    greet(colp + around + zp + [twin, far, diag])

    ng_copies = [
        remote(ng.at[colb[k]], ng_in.at[k], ng_s.at[k], ng_r.at[k], colp[k])
        for k in range(N_COL - 1)
    ]
    for c in ng_copies:
        c.start()
    pair_copies = [
        remote(down.at[1 - core], down0, c_s.at[0], c_r.at[0], twin),
        remote(up.at[1 - core], up0, c_s.at[1], c_r.at[1], twin),
    ]
    for c in pair_copies:
        c.start()
    part_copies = [
        remote(part.at[colb[k]], part_in.at[k], part_s.at[k], part_r.at[k], colp[k])
        for k in range(N_COL - 1)
    ]
    for c in part_copies:
        c.start()

    for c in pair_copies:
        c.wait_recv()
    for k in range(NZ):
        down_h[k] = (down[core, k].astype(F32) + down0[k].astype(F32)).astype(BF16)
        up_h[k] = (up[core, k].astype(F32) + up0[k].astype(F32)).astype(BF16)
    z_copies = []
    for k in range(NZ - 1):
        z_copies.append(
            remote(down_h.at[zb[k]], down1.at[k], z_s.at[0, k], z_r.at[0, k], zp[k])
        )
        z_copies.append(remote(up_h.at[zb[k]], up1.at[k], z_s.at[1, k], z_r.at[1, k], zp[k]))
    for c in z_copies:
        c.start()

    for c in ng_copies:
        c.wait_recv()
    total = ng[col].astype(F32)
    for k in range(N_COL - 1):
        total = total + ng_in[k].astype(F32)
    m = mixed[...]
    centred = m - jnp.mean(m, axis=-1, keepdims=True)
    inv = lax.rsqrt(jnp.mean(centred * centred, axis=-1, keepdims=True) + 1e-06)
    hat = centred * inv
    dy = total * gain[...]
    dm = inv * (
        dy - jnp.mean(dy, axis=-1, keepdims=True) - hat * jnp.mean(dy * hat, axis=-1, keepdims=True)
    )
    dm = dm.astype(BF16).astype(F32)
    for g in range(SUB):
        flat[pl.ds(g, PIX, stride=16)] = dm[:, g * LANE : (g + 1) * LANE]
    for i in range(ROWS):
        for j in range(COLS):
            v = flat[pl.ds((i * COLS + j) * 16, SUB)]
            mgpad[3 + i, 3 + j] = v.astype(BF16)
            mwide[i, j] = v
    halo = halo_copies(mgpad, row, col, halo_s, halo_r)
    for c in halo:
        c.start()

    widen(pad, wide, row, col)

    def taps(p, _):
        acc = [jnp.zeros((SUB, LANE), F32) for _ in range(7)]
        for i in range(ROWS):
            line = wide[i + p]
            mine = mwide[i]
            for q in range(7):
                acc[q] = acc[q] + jnp.sum(line[q : q + COLS] * mine, axis=0)
        for q in range(7):
            t = p * 7 + q
            ker[t // 4, lax.rem(t, 4)] = acc[q].astype(BF16)
        return 0

    lax.fori_loop(0, 7, taps, 0)
    for t in range(49, 64):
        ker[t // 4, t % 4] = jnp.zeros((SUB, LANE), BF16)
    k1 = [
        remote(ker.at[colb[k]], ker_in.at[k], k1_s.at[k], k1_r.at[k], colp[k])
        for k in range(N_COL - 1)
    ]
    for c in k1:
        c.start()

    for c in z_copies:
        c.wait_recv()
    ds, us = down_h[z].astype(F32), up_h[z].astype(F32)
    for k in range(NZ - 1):
        ds = ds + down1[k].astype(F32)
        us = us + up1[k].astype(F32)
    down_c[...] = ds.astype(BF16)
    up_c[...] = us.astype(BF16)
    h_copies = [
        remote(down_c, down2, h_s.at[0], h_r.at[0], far),
        remote(up_c, up2, h_s.at[1], h_r.at[1], far),
    ]
    for c in h_copies:
        c.start()

    for c in k1:
        c.wait_recv()
    ks = ker[col].astype(F32)
    for k in range(N_COL - 1):
        ks = ks + ker_in[k].astype(F32)
    ker_z[z] = ks
    k2 = [
        remote(ker_z.at[z], ker_z.at[z], k2_s.at[k], k2_r.at[k], zp[k]) for k in range(NZ - 1)
    ]
    for c in k2:
        c.start()

    for c in halo:
        c.wait_recv()
    widen(mgpad, wide, row, col)

    def line(i, _):
        gin[i] = (row_of_taps(wide, kern, i, True) + og[i]).astype(BF16)
        return 0

    lax.fori_loop(0, ROWS, line, 0)

    for c in h_copies:
        c.wait_recv()
    gdown[core, z] = (down_c[...].astype(F32) + down2[...].astype(F32)).astype(BF16)
    gup[core, z] = (up_c[...].astype(F32) + up2[...].astype(F32)).astype(BF16)
    a_copies = []
    for k in range(NZ - 1):
        a_copies.append(
            remote(gdown.at[core, z], gdown.at[core, z], a_s.at[0, k], a_r.at[0, k], zp[k])
        )
        a_copies.append(remote(gup.at[core, z], gup.at[core, z], a_s.at[1, k], a_r.at[1, k], zp[k]))
    for c in a_copies:
        c.start()

    def across(ref, n, k, zz, cc):
        return remote(ref.at[cc, zz], ref.at[cc, zz], b_s.at[n, k], b_r.at[n, k], twin)

    across(gdown, 0, NZ - 1, z, core).start()
    across(gup, 1, NZ - 1, z, core).start()

    for c in k2:
        c.wait_recv()
    ks = ker_z[0]
    for k in range(1, NZ):
        ks = ks + ker_z[k]
    ker_q[yh * NC + core] = ks
    q = yh * NC + core
    k3 = [
        remote(ker_q.at[q], ker_q.at[q], k3_s.at[n], k3_r.at[n], where)
        for n, where in enumerate((twin, far, diag))
    ]
    for c in k3:
        c.start()

    for c in part_copies:
        c.wait_recv()
    tok = part[col].astype(F32)
    for k in range(N_COL - 1):
        tok = tok + part_in[k].astype(F32)
    seq[...] = jnp.where(slot[...] >= 0, tok.astype(BF16).astype(F32), text[...]).astype(BF16)

    for c in k3:
        c.wait_recv()
    ker_out[col] = (ker_q[0] + ker_q[1] + ker_q[2] + ker_q[3]).astype(BF16)
    k4 = [
        remote(ker_out.at[col], ker_out.at[col], k4_s.at[k], k4_r.at[k], colp[k])
        for k in range(N_COL - 1)
    ]
    for c in k4:
        c.start()
    for k in range(NZ - 1):
        for n, ref in enumerate((gdown, gup)):
            block = ref.at[core, zf[k]]
            remote(block, block, a_s.at[n, k], a_r.at[n, k], zp[k]).wait_recv()
            across(ref, n, k, zf[k], core).start()
    for k in range(N_COL - 1):
        block = ker_out.at[colf[k]]
        remote(block, block, k4_s.at[k], k4_r.at[k], colp[k]).wait_recv()
    for t in range(49):
        gker[t] = ker_out[t // 4, t % 4].astype(F32)
    for n, ref in enumerate((gdown, gup)):
        for k in range(NZ - 1):
            across(ref, n, k, zf[k], 1 - core).wait_recv()
        across(ref, n, NZ - 1, z, 1 - core).wait_recv()
        for k in range(NZ - 1):
            across(ref, n, k, zf[k], core).wait_send()
        across(ref, n, NZ - 1, z, core).wait_send()
    for c in ng_copies + pair_copies + part_copies + z_copies + halo + k1 + h_copies + k2:
        c.wait_send()
    for c in a_copies + k3 + k4:
        c.wait_send()


def backward(ng, part, up, down, mixed, gain, kern, pad, og, slot, text):
    vm = pl.BlockSpec(memory_space=pltpu.VMEM)
    dma = pltpu.SemaphoreType.DMA
    v = pltpu.VMEM
    w = D // NZ // NC
    h = HID // NZ // NC
    return pl.pallas_call(
        backward_kernel,
        out_shape=(
            jax.ShapeDtypeStruct((SLOT_PAD, D), BF16),
            jax.ShapeDtypeStruct((ROWS, COLS, SUB, LANE), BF16),
            jax.ShapeDtypeStruct((49, SUB, LANE), F32),
            jax.ShapeDtypeStruct((NC, NZ, w, HID), BF16),
            jax.ShapeDtypeStruct((NC, NZ, h, D), BF16),
        ),
        in_specs=[vm] * 11,
        out_specs=[vm] * 5,
        scratch_shapes=[
            v((N_COL - 1, PIX, D), BF16),
            v((N_COL - 1, SLOT_PAD, D), BF16),
            v((NZ, w, HID), BF16), v((NZ, h, D), BF16),
            v((NZ - 1, w, HID), BF16), v((NZ - 1, h, D), BF16),
            v((w, HID), BF16), v((h, D), BF16),
            v((NZ, w, HID), BF16), v((NZ, h, D), BF16),
            v((w, HID), BF16), v((h, D), BF16),
            v((ROWS + 6, COLS + 6, SUB, LANE), BF16),
            v((ROWS + 6, COLS + 6, SUB, LANE), F32),
            v((ROWS, COLS, SUB, LANE), F32),
            v((PIX * 16, LANE), F32),
            v((16, 4, SUB, LANE), BF16),
            v((N_COL - 1, 4, SUB, LANE), BF16),
            v((NZ, 4, SUB, LANE), F32),
            v((4, 4, SUB, LANE), F32),
            v((16, 4, SUB, LANE), BF16),
            dma((15,)), dma((15,)), dma((15,)), dma((15,)), dma((8,)), dma((8,)),
            dma((2,)), dma((2,)), dma((2, 7)), dma((2, 7)), dma((2,)), dma((2,)),
            dma((2, 7)), dma((2, 7)), dma((2, 8)), dma((2, 8)),
            dma((15,)), dma((15,)), dma((7,)), dma((7,)), dma((3,)), dma((3,)),
            dma((15,)), dma((15,)),
        ],
        compiler_params=pltpu.CompilerParams(
            collective_id=1, has_side_effects=True, vmem_limit_bytes=VMEM_LIMIT
        ),
    )(ng, part, up, down, mixed, gain, kern, pad, og, slot, text)


def gelu_tanh(value):
    return jax.nn.gelu(value, approximate=True)


def local(
    features, kernel, ln_gain, ln_bias, w_up, b_up, w_down, layer_scale,
    text_embed, slot_token, seq_grad,
):
    me = lax.axis_index("col")
    kern = kernel.reshape(49, SUB, LANE)
    feat = features.reshape(ROWS, COLS, SUB, LANE)
    gain, bias = ln_gain.reshape(1, D), ln_bias.reshape(1, D)
    tail = jnp.pad(slot_token.astype(BF16).reshape(1, SLOTS), ((0, 3), (0, D - SLOTS)))
    slots = jnp.concatenate([seq_grad, tail], axis=0)
    normed, slots_all, mixed, pad = forward(feat, kern, gain, bias, slots)

    band = normed.reshape(N_COL * PIX, D)
    held = slots_all[:, SLOTS, :SLOT_PAD].astype(jnp.int32)
    held = jnp.where(lax.broadcasted_iota(jnp.int32, held.shape, 1) < SLOTS, held, -1)
    pix = np.arange(PIX)
    inner = (pix // COLS // 2) * 3 + (pix % COLS) // 2
    token = (np.arange(N_COL)[:, None] * 6 + inner[None, :]).reshape(-1)
    select = (jnp.asarray(token, jnp.int32)[:, None] == held.reshape(-1)[None, :]).astype(BF16)
    mine = (
        (jnp.asarray(inner, jnp.int32)[:, None] + me * 6) == held.reshape(-1)[None, :]
    ).astype(BF16)
    every = slots_all.reshape(N_COL * SLOT_PAD, D)
    out_grad = jnp.dot(select, every, preferred_element_type=F32) * 0.25
    bg = (layer_scale * out_grad).astype(BF16)
    og = (jnp.dot(mine, every, preferred_element_type=F32) * 0.25).reshape(ROWS, COLS, SUB, LANE)
    pre = jnp.dot(band, w_up, preferred_element_type=F32) + b_up
    act = gelu_tanh(pre).astype(BF16)
    act_grad = jnp.einsum("pd,hd->ph", bg, w_down, preferred_element_type=F32)
    pre_grad = jax.vjp(gelu_tanh, pre)[1](act_grad)[0].astype(BF16)
    ng = jnp.einsum("ph,dh->pd", pre_grad, w_up, preferred_element_type=F32).astype(BF16)
    down = jnp.einsum("ph,pd->hd", act, bg, preferred_element_type=F32).astype(BF16)
    up = jnp.einsum("pd,ph->dh", band, pre_grad, preferred_element_type=F32).astype(BF16)
    pooled = (jnp.einsum("ps,ph->sh", select, act, preferred_element_type=F32) * 0.25).astype(BF16)
    part = layer_scale * jnp.dot(pooled, w_down, preferred_element_type=F32)
    part = part + 0.25 * jnp.einsum(
        "ps,pd->sd", mine, features.reshape(PIX, D), preferred_element_type=F32
    )
    part = part.astype(BF16)

    slot = jnp.pad(slot_token, (0, SLOT_PAD - SLOTS), constant_values=-1)[:, None]
    text = jnp.pad(text_embed.astype(F32), ((0, SLOT_PAD - SLOTS), (0, 0)))
    seq, gin, gker, gup, gdown = backward(
        ng.reshape(N_COL, PIX, D),
        part.reshape(N_COL, SLOT_PAD, D),
        up.reshape(NC, NZ, D // NC // NZ, HID),
        down.reshape(NC, NZ, HID // NC // NZ, D),
        mixed, gain, kern, pad, og,
        jnp.broadcast_to(slot, (SLOT_PAD, D)), text,
    )
    return (
        seq[:SLOTS],
        gin.reshape(ROWS, COLS, D),
        gker.reshape(49, D),
        gup.reshape(D, HID),
        gdown.reshape(HID, D),
    )


def solution(mesh):
    placed = (
        P("row", "col", None), P(), P(), P(), P(None, "col"), P("col"), P("col", None), P(),
        P(("row", "col"), None), P(("row", "col")), P(("row", "col"), None),
    )
    return jax.shard_map(
        local,
        mesh=mesh,
        in_specs=placed,
        out_specs=(
            P(("row", "col"), None), P("row", "col", None), P(), P(None, "col"), P("col", None),
        ),
        check_vma=False,
    )
```

time: 1060 us -> 165 us (0.16)
  waiting for transfers between devices: 877 us -> 0 us
  Pallas kernels: 0 us -> 133 us
  blocking collectives: 73.4 us -> 0 us
  starting transfers between devices: 44.2 us -> 0 us
  between operations: 16.9 us -> 0.93 us
    psum x2 -> x0, waiting for transfers between devices: 574 us -> none  [the longest x1 304 us: local(): lax.psum(up_local.astype(jnp.bfloat16), 'row').astype(jnp.float32)]
    all_gather x2 -> x0, waiting for transfers between devices: 148 us -> none  [the longest x1 82.8 us: local(): lax.all_gather(normed.reshape(pixels, chans), 'col', axis=0, tiled=True)]
    reduce_scatter x2 -> x0, waiting for transfers between devices: 148 us -> none  [the longest x1 79 us: local(): lax.psum_scatter(jnp.einsum('ph,dh->pd', piece, w_up, preferred_element_t...]
    pallas_call x0 -> x2, Pallas kernels: none -> 133 us  [the longest x1 86.1 us: backward(): pl.pallas_call(backward_kernel, out_shape=(jax.ShapeDtypeStruct((SLOT_PAD...]
    unnamed x1 -> x0, blocking collectives: 40.3 us -> none
    ppermute x8 -> x0, starting transfers between devices: 38.6 us -> none  [the longest x4 32.2 us: with_halo(): lax.ppermute(tail, axis, [(i, (i + 1) % count) for i in range(ends)])]
    all_gather x1 -> x0, blocking collectives: 33.1 us -> none  [local(): band_tokens = lax.all_gather(tokens, 'col', axis=0, tiled=True)]
  transfers between devices with their start and end apart: 18 -> 0, of which waited for: 9 -> 0; matrix products, arithmetic and copies ran while one was open for 3% -> 0% of each run, Pallas kernels for 0% -> 0%
where the time goes in v1:
time: 165 us; the launch traced here: 164 us
  Pallas kernels  133 us (81%)
  local copies, waits for them, and re-layouts  17.2 us (10%)
  matrix products  9.11 us (6%)
  other arithmetic  4.41 us (3%)
    pallas_call x1, Pallas kernels, backward(): pl.pallas_call(backward_kernel, out_shape=(jax.ShapeDtypeStruct((SLOT_PAD...  86.1 us
    pallas_call x1, Pallas kernels, forward(): pl.pallas_call(forward_kernel, out_shape=(jax.ShapeDtypeStruct((N_COL, PI...  46.5 us
    unnamed x50, local copies, waits for them, and re-layouts  10.2 us

profile of v1, /device:TPU:1, one launch (start us, length us, event | category | flops | bytes accessed | tf_op | source)
XLA Modules:
  0.0 164.2 jit_solution(11210539655840830881)
XLA Ops:
  0.7 0.8 broadcast_add_fusion
  2.8 0.7 reshape.83.gain
  3.5 0.7 reshape.84.bias
  4.2 0.7 broadcast_multiply_fusion
  4.9 0.8 fusion.22.slots
  5.8 0.7 broadcast_in_dim.7.slot
  6.5 1.4 pad_convert_fusion.text
  7.9 0.9 copy.21
  9.5 0.9 reshape.81
  10.5 46.5 %shard_map.164 = (bf16[16,24,1536]{2,1,0:T(8,128)(2,1)S(1)}, bf16[16,16,1536]{2,1,0:T(8,128)(2,1)S(1)}, f32[24,1536]{1,0:T(8,128)S(1)}, bf16[10,12,12,128]{3,2,1,0:T(8,128)(2,1)S(1)}) custom-call(bf16[4,6,12,128]{3,2,1,0:T(8,128)(2,1)S(1)} %copy.20.feat, f32[49,12,128]{2,1,0:T(8,128)S(1)} %reshape.82.kern, f32[1,1536]{1,0:T(1,128)S(1)} %reshape.83.gain, ...), custom_call_target="tpu_custom_call" | custom-call | tf_op jit(solution)/shard_map/pallas_call | solution.py:160
  57.1 0.8 copy-done.3
  58.9 0.7 reshape.93.og
  62.8 0.7 copy-done.14
  63.5 1.5 convolution_convert_fusion.2
  65.0 1.5 convolution_convert_fusion
  66.6 2.0 %convolution_multiply_fusion.2 = f32[256,1536]{1,0:T(8,128)S(1)} fusion(bf16[256,1536]{1,0:T(8,128)(2,1)} %param.19, f32[1536]{0:T(1024)} %param.20, s32[256]{0:T(256)} %copy-done.18, s32[384]{0:T(512)} %constant.36.clone, f32[384,256]{1,0:T(8,128)} %copy-done.16), kind=kOutput, calls=%fused_computation.4 | convolution fusion | flops 253165568 | bytes 2761216 | tf_op jit(solution)/shard_map/dot_general | solution.py:485
  68.6 1.5 fusion.2
  70.2 86.1 %shard_map.165 = (bf16[16,1536]{1,0:T(8,128)(2,1)S(1)}, bf16[4,6,12,128]{3,2,1,0:T(8,128)(2,1)S(1)}, f32[49,12,128]{2,1,0:T(8,128)S(1)}, bf16[2,8,96,256]{3,2,1,0:T(8,128)(2,1)S(1)}, bf16[2,8,16,1536]{3,2,1,0:T(8,128)(2,1)S(1)}) custom-call(bf16[16,24,1536]{2,1,0:T(8,128)(2,1)} %bitcast.39, bf16[16,16,1536]{2,1,0:T(8,128)(2,1)S(1)} %bitcast.31, ...), custom_call_target="tpu_custom_call" | custom-call | tf_op jit(solution)/shard_map/pallas_call | solution.py:407
  156.3 0.7 copy-done.5
  158.3 1.0 reshape.99
  160.0 1.0 pad.21
  161.0 0.8 copy.24
  162.5 0.9 copy.29
  163.4 0.9 copy.30
  (59 shorter events, 9.0 us)
Async XLA Ops:
  0.6 60.6 %copy-start = (bf16[1536,256]{1,0:T(8,128)(2,1)S(1)}, bf16[1536,256]{1,0:T(8,128)(2,1)}, u32[]{:S(2)}) copy-start(bf16[1536,256]{1,0:T(8,128)(2,1)} %param.17) | copy-start | bytes 2359300
  0.6 9.8 %copy-start.17 = (f32[49,1536]{1,0:T(8,128)S(1)}, f32[49,1536]{1,0:T(8,128)}, u32[]{:S(2)}) copy-start(f32[49,1536]{1,0:T(8,128)} %param.14) | copy-start | bytes 903172
  1.4 57.2 %copy-start.20 = (s32[24]{0:T(128)}, s32[24]{0:T(128)S(1)}, u32[]{:S(2)}) copy-start(s32[24]{0:T(128)S(1)} %broadcast_add_fusion) | copy-start | bytes 292
  10.4 49.2 %copy-start.19 = (s32[384]{0:T(512)S(1)}, s32[384]{0:T(512)}, u32[]{:S(2)}) copy-start(s32[384]{0:T(512)} %constant.36.clone) | copy-start | bytes 4612
  57.1 0.8 copy-start.3
  57.8 0.7 copy-start.8
  58.5 2.8 %copy-start.13 = (bf16[16,24,1536]{2,1,0:T(8,128)(2,1)}, bf16[16,24,1536]{2,1,0:T(8,128)(2,1)S(1)}, u32[]{:S(2)}) copy-start(bf16[16,24,1536]{2,1,0:T(8,128)(2,1)S(1)} %get-tuple-element.15) | copy-start | bytes 3538948
  58.6 1.5 copy-start.18
  59.6 1.1 copy-start.15
  60.7 0.7 copy-start.21
  62.1 0.7 copy-start.16
  62.1 1.4 copy-start.14
  68.6 1.6 copy-start.1
  68.6 1.6 copy-start.2
  68.6 1.6 copy-start.4
  68.6 1.6 copy-start.6
  68.6 1.6 copy-start.7
  68.6 1.6 copy-start.9
  156.3 0.8 copy-start.5
  157.1 0.6 copy-start.10
  157.7 0.6 copy-start.11
  158.3 3.6 %copy-start.12 = (bf16[16,1536]{1,0:T(8,128)(2,1)S(1)}, bf16[16,1536]{1,0:T(8,128)(2,1)}, u32[]{:S(2)}) copy-start(bf16[16,1536]{1,0:T(8,128)(2,1)} %copy-done.11) | copy-start | bytes 147460

commit v2 on v1

v2 whole, which is shorter than its diff:
```python
import jax
import jax.numpy as jnp
from jax import lax
from jax.experimental import pallas as pl
from jax.experimental.pallas import tpu as pltpu
from jax.sharding import PartitionSpec as P

F32, BF16 = jnp.float32, jnp.bfloat16
D, LANE, SUB = 1536, 128, 12
ROWS, COLS, PIX, SLOTS, SLOT_PAD = 4, 6, 24, 12, 16
N_ROW, N_COL = 32, 16
NX, NY = 4, 4
NZ, NC = 8, 2
HID = 256
DIRS = [(a, b) for a in (-1, 0, 1) for b in (-1, 0, 1) if (a, b) != (0, 0)]
MESH = pl.DeviceIdType.MESH
VMEM_LIMIT = 48 * 1024 * 1024
SRC_ROW = {1: (1, 3), 0: (0, 4), -1: (0, 3)}
DST_ROW = {1: 0, 0: 3, -1: 7}
SRC_COL = {1: (3, 3), 0: (0, 6), -1: (0, 3)}
DST_COL = {1: 0, 0: 3, -1: 9}


def remote(src, dst, send, recv, where):
    return pltpu.make_async_remote_copy(
        src_ref=src, dst_ref=dst, send_sem=send, recv_sem=recv, device_id=where, device_id_type=MESH
    )


def greet(where):
    barrier = pltpu.get_barrier_semaphore()
    for device in where:
        pl.semaphore_signal(barrier, inc=1, device_id=device, device_id_type=MESH)
    pl.semaphore_wait(barrier, len(where))


def halo_copies(pad, row, col, send, recv):
    out = []
    for k, (a, b) in enumerate(DIRS):
        r0, nr = SRC_ROW[a]
        c0, nc = SRC_COL[b]
        where = (lax.rem(row + a + N_ROW, N_ROW), lax.rem(col + b + N_COL, N_COL))
        out.append(
            remote(
                pad.at[pl.ds(3 + r0, nr), pl.ds(3 + c0, nc)],
                pad.at[pl.ds(DST_ROW[a], nr), pl.ds(DST_COL[b], nc)],
                send.at[k],
                recv.at[k],
                where,
            )
        )
    return out


def widen(pad, wide, row, col):
    top = jnp.where(row == 0, 0.0, 1.0)
    bottom = jnp.where(row == N_ROW - 1, 0.0, 1.0)
    left = jnp.where(col == 0, 0.0, 1.0)
    right = jnp.where(col == N_COL - 1, 0.0, 1.0)
    for a in range(ROWS + 6):
        edge = top if a < 3 else bottom if a >= 7 else 1.0
        wide[a, pl.ds(0, 3)] = pad[a, pl.ds(0, 3)].astype(F32) * (edge * left)
        if a < 3 or a >= 7:
            wide[a, pl.ds(3, 6)] = pad[a, pl.ds(3, 6)].astype(F32) * edge
        else:
            wide[a, pl.ds(3, 6)] = pad[a, pl.ds(3, 6)].astype(F32)
        wide[a, pl.ds(9, 3)] = pad[a, pl.ds(9, 3)].astype(F32) * (edge * right)


def row_of_taps(wide, kern, i, flip):
    def step(p, acc):
        line = wide[i + (6 - p if flip else p)]
        for q in range(7):
            s = 6 - q if flip else q
            tap = kern[pl.ds(pl.multiple_of((p * 7 + q) * 16, 16), SUB)]
            acc = acc + line[s : s + COLS] * tap
        return acc

    return lax.fori_loop(0, 7, step, jnp.zeros((COLS, SUB, LANE), F32))


def dot(a, b, ca, cb):
    return lax.dot_general(a, b, (((ca,), (cb,)), ((), ())), preferred_element_type=F32)


def whole_kernel(
    feat, kern, small, slots, w_up, w_down, text,
    seq, gin, gker, gup, gdown,
    pad, wide, flat, kflat, feat2, mixed, normed, band, every, select, bg, og, act_grad,
    act, pre_grad, ng, ng_x, ng_t, ng_y, part, part_x, part_t, part_y,
    up, down, up0, down0, up1, down1, up2, down2, up_h, down_h, up_c, down_c,
    mgpad, mwide, ker, ker_in, ker_z, ker_q, ker_out,
    f_s, f_r, n_s, n_r, g_s, g_r, nx_s, nx_r, ny_s, ny_r, px_s, px_r, py_s, py_r, halo_s, halo_r,
    c_s, c_r, z_s, z_r, h_s, h_r, a_s, a_r, b_s, b_r, k1_s, k1_r, k2_s, k2_r, k3_s, k3_r, k4_s, k4_r,
):
    row, col = lax.axis_index("row"), lax.axis_index("col")
    y, x = col // NX, lax.rem(col, NX)
    core = lax.rem(row, NC)
    z = lax.rem(row // NC, NZ)
    yh = row // (NC * NZ)
    at = lambda yy, zz, cc: ((yy * NZ + zz) * NC + cc, col)
    peer = lambda dy, dx: lax.rem(y + dy + NY, NY) * NX + lax.rem(x + dx + NX, NX)
    yp = [(row, peer(dy, 0)) for dy in range(1, NY)]
    xp = [(row, peer(0, dx)) for dx in range(1, NX)]
    colp = [(row, lax.rem(col + k, N_COL)) for k in range(1, N_COL)]
    colb = [lax.rem(col + k, N_COL) for k in range(1, N_COL)]
    colf = [lax.rem(col - k + N_COL, N_COL) for k in range(1, N_COL)]
    zb = [lax.rem(z + k, NZ) for k in range(1, NZ)]
    zf = [lax.rem(z - k + NZ, NZ) for k in range(1, NZ)]
    zp = [at(yh, k, core) for k in zb]
    twin = at(yh, z, 1 - core)
    far = at(1 - yh, z, core)
    diag = at(1 - yh, z, 1 - core)
    around = [
        (lax.rem(row + a + N_ROW, N_ROW), lax.rem(col + b + N_COL, N_COL)) for a, b in DIRS
    ]
    gain, bias, scale = small[0:1], small[1:2], small[2:3]
    slot_rows = lambda d: pl.ds(pl.multiple_of(d * SLOT_PAD, SLOT_PAD), SLOT_PAD)

    pad[pl.ds(3, ROWS), pl.ds(3, COLS)] = feat[...]
    every[slot_rows(col)] = slots[...]
    for g in range(SUB):
        kflat[pl.ds(g, 49, stride=16)] = kern[:, g * LANE : (g + 1) * LANE]
    for i in range(ROWS):
        for j in range(COLS):
            flat[pl.ds((i * COLS + j) * 16, SUB)] = feat[i, j].astype(F32)
    feat2[...] = jnp.zeros_like(feat2)
    for g in range(SUB):
        feat2[pl.ds(0, PIX), pl.ds(g * LANE, LANE)] = flat[pl.ds(g, PIX, stride=16)]
    greet(around + colp + zp + [twin, far, diag])

    f_halo = halo_copies(pad, row, col, f_s, f_r)
    for c in f_halo:
        c.start()

    n_at = lambda d: normed.at[d]
    g_at = lambda d: every.at[slot_rows(d)]

    def own(at_, send, recv):
        out = []
        for dy in range(1, NY):
            out.append(remote(at_(col), at_(col), send.at[dy, 0], recv.at[dy, 0], yp[dy - 1]))
        for dx in range(1, NX):
            out.append(remote(at_(col), at_(col), send.at[0, dx], recv.at[0, dx], xp[dx - 1]))
        return out

    def passed(at_, send, recv, dy, dx):
        b = peer(-dy, 0)
        return remote(at_(b), at_(b), send.at[dy, dx], recv.at[dy, dx], xp[dx - 1])

    def came(at_, send, recv, dy, dx):
        b = peer(-dy, -dx)
        return remote(at_(b), at_(b), send.at[dy, dx], recv.at[dy, dx], (row, peer(dy, dx)))

    g_all, n_all = (g_at, g_s, g_r), (n_at, n_s, n_r)

    def onward(ref):
        for dy in range(1, NY):
            came(*ref, dy, 0).wait_recv()
            for dx in range(1, NX):
                passed(*ref, dy, dx).start()

    def arrived(ref):
        for dx in range(1, NX):
            for dy in range(NY):
                came(*ref, dy, dx).wait_recv()

    for c in own(*g_all):
        c.start()
    for c in f_halo:
        c.wait_recv()
    onward(g_all)
    widen(pad, wide, row, col)

    def line(i, _):
        acc = row_of_taps(wide, kflat, i, False)
        for j in range(COLS):
            flat[pl.ds(pl.multiple_of((i * COLS + j) * 16, 16), SUB)] = acc[j]
        return 0

    lax.fori_loop(0, ROWS, line, 0)
    for g in range(SUB):
        mixed[:, pl.ds(g * LANE, LANE)] = flat[pl.ds(g, PIX, stride=16)]
    m = mixed[...]
    centred = m - jnp.mean(m, axis=-1, keepdims=True)
    var = jnp.mean(centred * centred, axis=-1, keepdims=True)
    normed[col] = (centred * lax.rsqrt(var + 1e-06) * gain + bias).astype(BF16)
    for c in own(*n_all):
        c.start()
    onward(n_all)

    arrived(g_all)
    names = jnp.zeros((SLOT_PAD, 256), F32)
    for d in range(N_COL):
        names = names + every[pl.ds(d * SLOT_PAD, SLOT_PAD), pl.ds(0, 256)].astype(F32)
    names = names[SLOTS : SLOTS + 1] - 1.0

    def token_of(count, first):
        p = lax.broadcasted_iota(jnp.int32, (count, 1), 0)
        d = jnp.where(p >= PIX, 1, 0)
        p = p - d * PIX
        one = lambda c: jnp.where(c, 1, 0)
        i = one(p >= 6) + one(p >= 12) + one(p >= 18)
        j = p - i * COLS
        t = 3 * one(i >= 2) + one(j >= 2) + one(j >= 4)
        return ((first + d) * 6 + t).astype(F32)

    for d in range(0, N_COL, 2):
        hit = token_of(2 * PIX, d) == names
        select[pl.ds(d * PIX, 2 * PIX)] = jnp.where(hit, 1.0, 0.0).astype(BF16)
    p32 = lax.broadcasted_iota(jnp.int32, (32, 1), 0)
    hit = jnp.where(p32 < PIX, token_of(32, col), -9.0) == names
    mine = jnp.where(hit, 1.0, 0.0).astype(BF16)

    def grads(c, _):
        cut = pl.ds(pl.multiple_of(c * 512, 512), 512)
        g = dot(select[...], every[:, cut], 1, 0) * 0.25
        bg[:, cut] = (g * small[2:3, cut]).astype(BF16)
        og[:, cut] = dot(mine, every[:, cut], 1, 0) * 0.25
        return 0

    lax.fori_loop(0, 3, grads, 0)

    def hidden_grads(r, _):
        cut = pl.ds(pl.multiple_of(r * 128, 128), 128)
        act_grad[cut] = dot(bg[cut], w_down[...], 1, 1)
        return 0

    lax.fori_loop(0, 3, hidden_grads, 0)

    arrived(n_all)
    for d in range(0, N_COL, 2):
        two = jnp.concatenate([normed[d].astype(F32), normed[d + 1].astype(F32)], axis=0)
        band[pl.ds(d * PIX, 2 * PIX)] = two.astype(BF16)

    def hidden(r, _):
        cut = pl.ds(pl.multiple_of(r * 128, 128), 128)
        v = dot(band[cut], w_up[...], 1, 0) + small[3:4, 0:HID]
        k0, k1 = 0.7978845608028654, 0.044715
        t = jnp.tanh(k0 * (v + k1 * v * v * v))
        act[cut] = (0.5 * v * (1.0 + t)).astype(BF16)
        slope = 0.5 * (1.0 + t) + 0.5 * v * (1.0 - t * t) * (k0 * (1.0 + 3.0 * k1 * v * v))
        pre_grad[cut] = (act_grad[cut] * slope).astype(BF16)
        return 0

    lax.fori_loop(0, 3, hidden, 0)

    def back(c, _):
        cut = pl.ds(pl.multiple_of(c * 512, 512), 512)
        v = dot(pre_grad[...], w_up[cut], 1, 1)
        for d in range(N_COL):
            ng[d, :, cut] = v[d * PIX : (d + 1) * PIX].astype(BF16)
        return 0

    lax.fori_loop(0, 3, back, 0)

    def across_x(at_, to, send, recv):
        out = {}
        for dy in (1, 2, 3, 0):
            for dx in range(1, NX):
                out[dy, dx] = remote(
                    at_(peer(dy, dx)), to.at[dx - 1, dy], send.at[dx, dy], recv.at[dx, dy],
                    xp[dx - 1],
                )
        return out

    def along_y(at_, xs, came_x, held, to, send, recv):
        out = []
        for dy in range(1, NY):
            v = at_(peer(dy, 0))[...].astype(F32)
            for dx in range(1, NX):
                xs[dy, dx].wait_recv()
                v = v + came_x[dx - 1, dy].astype(F32)
            held[dy - 1] = v.astype(BF16)
            out.append(
                remote(held.at[dy - 1], to.at[dy - 1], send.at[dy - 1], recv.at[dy - 1], yp[dy - 1])
            )
            out[-1].start()
        return out

    def at_home(at_, xs, came_x, ys, came_y):
        v = at_(col)[...].astype(F32)
        for dx in range(1, NX):
            xs[0, dx].wait_recv()
            v = v + came_x[dx - 1, 0].astype(F32)
        for dy in range(1, NY):
            ys[dy - 1].wait_recv()
            v = v + came_y[dy - 1].astype(F32)
        return v

    ng_at = lambda d: ng.at[d]
    ng_xs = across_x(ng_at, ng_x, nx_s, nx_r)
    for c in ng_xs.values():
        c.start()

    def down_part(c, _):
        cut = pl.ds(pl.multiple_of(c * 512, 512), 512)
        v = dot(act[...], bg[:, cut], 0, 0)
        for k in range(NC * NZ):
            down[k // NZ, k % NZ, :, cut] = v[k * 16 : (k + 1) * 16].astype(BF16)
        return 0

    lax.fori_loop(0, 3, down_part, 0)
    pair = [
        remote(down.at[1 - core], down0, c_s.at[0], c_r.at[0], twin),
        remote(up.at[1 - core], up0, c_s.at[1], c_r.at[1], twin),
    ]
    pair[0].start()
    for c in range(4):
        v = dot(band[:, c * 384 : (c + 1) * 384], pre_grad[...], 0, 0)
        for k in range(4):
            b = c * 4 + k
            up[b // NZ, b % NZ] = v[k * 96 : (k + 1) * 96].astype(BF16)
    pair[1].start()

    pooled = (dot(select[...], act[...], 0, 0) * 0.25).astype(BF16)

    def tokens(c, _):
        cut = pl.ds(pl.multiple_of(c * 512, 512), 512)
        v = dot(pooled, w_down[:, cut], 1, 0) * small[2:3, cut]
        v = v + 0.25 * dot(mine, feat2[:, cut].astype(BF16), 0, 0)
        part[:, cut] = v.astype(BF16)
        return 0

    lax.fori_loop(0, 3, tokens, 0)
    part_at = lambda d: part.at[slot_rows(d)]
    part_xs = across_x(part_at, part_x, px_s, px_r)
    for c in part_xs.values():
        c.start()

    for c in pair:
        c.wait_recv()
    for k in range(NZ):
        down_h[k] = (down[core, k].astype(F32) + down0[k].astype(F32)).astype(BF16)
        up_h[k] = (up[core, k].astype(F32) + up0[k].astype(F32)).astype(BF16)
    z_copies = []
    for k in range(NZ - 1):
        z_copies.append(
            remote(down_h.at[zb[k]], down1.at[k], z_s.at[0, k], z_r.at[0, k], zp[k])
        )
        z_copies.append(remote(up_h.at[zb[k]], up1.at[k], z_s.at[1, k], z_r.at[1, k], zp[k]))
    for c in z_copies:
        c.start()

    ng_ys = along_y(ng_at, ng_xs, ng_x, ng_t, ng_y, ny_s, ny_r)
    total = at_home(ng_at, ng_xs, ng_x, ng_ys, ng_y)
    m = mixed[...]
    centred = m - jnp.mean(m, axis=-1, keepdims=True)
    inv = lax.rsqrt(jnp.mean(centred * centred, axis=-1, keepdims=True) + 1e-06)
    hat = centred * inv
    dy_ = total * gain
    dm = inv * (
        dy_
        - jnp.mean(dy_, axis=-1, keepdims=True)
        - hat * jnp.mean(dy_ * hat, axis=-1, keepdims=True)
    )
    dm = dm.astype(BF16).astype(F32)
    for g in range(SUB):
        flat[pl.ds(g, PIX, stride=16)] = dm[:, g * LANE : (g + 1) * LANE]
    for i in range(ROWS):
        for j in range(COLS):
            v = flat[pl.ds((i * COLS + j) * 16, SUB)]
            mgpad[3 + i, 3 + j] = v.astype(BF16)
            mwide[i, j] = v
    halo = halo_copies(mgpad, row, col, halo_s, halo_r)
    for c in halo:
        c.start()

    def taps(p, _):
        acc = [jnp.zeros((SUB, LANE), F32) for _ in range(7)]
        for i in range(ROWS):
            line = wide[i + p]
            own_line = mwide[i]
            for q in range(7):
                acc[q] = acc[q] + jnp.sum(line[q : q + COLS] * own_line, axis=0)
        for q in range(7):
            t = p * 7 + q
            ker[t // 4, lax.rem(t, 4)] = acc[q].astype(BF16)
        return 0

    lax.fori_loop(0, 7, taps, 0)
    for t in range(49, 64):
        ker[t // 4, t % 4] = jnp.zeros((SUB, LANE), BF16)
    k1 = [
        remote(ker.at[colb[k]], ker_in.at[k], k1_s.at[k], k1_r.at[k], colp[k])
        for k in range(N_COL - 1)
    ]
    for c in k1:
        c.start()
    part_ys = along_y(part_at, part_xs, part_x, part_t, part_y, py_s, py_r)

    for c in z_copies:
        c.wait_recv()
    ds, us = down_h[z].astype(F32), up_h[z].astype(F32)
    for k in range(NZ - 1):
        ds = ds + down1[k].astype(F32)
        us = us + up1[k].astype(F32)
    down_c[...] = ds.astype(BF16)
    up_c[...] = us.astype(BF16)
    h_copies = [
        remote(down_c, down2, h_s.at[0], h_r.at[0], far),
        remote(up_c, up2, h_s.at[1], h_r.at[1], far),
    ]
    for c in h_copies:
        c.start()

    for c in k1:
        c.wait_recv()
    ks = ker[col].astype(F32)
    for k in range(N_COL - 1):
        ks = ks + ker_in[k].astype(F32)
    ker_z[z] = ks
    k2 = [
        remote(ker_z.at[z], ker_z.at[z], k2_s.at[k], k2_r.at[k], zp[k]) for k in range(NZ - 1)
    ]
    for c in k2:
        c.start()

    for c in h_copies:
        c.wait_recv()
    gdown[core, z] = (down_c[...].astype(F32) + down2[...].astype(F32)).astype(BF16)
    gup[core, z] = (up_c[...].astype(F32) + up2[...].astype(F32)).astype(BF16)
    a_copies = []
    for k in range(NZ - 1):
        a_copies.append(
            remote(gdown.at[core, z], gdown.at[core, z], a_s.at[0, k], a_r.at[0, k], zp[k])
        )
        a_copies.append(remote(gup.at[core, z], gup.at[core, z], a_s.at[1, k], a_r.at[1, k], zp[k]))
    for c in a_copies:
        c.start()

    def across(ref, n, k, zz, cc):
        return remote(ref.at[cc, zz], ref.at[cc, zz], b_s.at[n, k], b_r.at[n, k], twin)

    across(gdown, 0, NZ - 1, z, core).start()
    across(gup, 1, NZ - 1, z, core).start()

    for c in k2:
        c.wait_recv()
    ks = ker_z[0]
    for k in range(1, NZ):
        ks = ks + ker_z[k]
    q = yh * NC + core
    ker_q[q] = ks
    k3 = [
        remote(ker_q.at[q], ker_q.at[q], k3_s.at[n], k3_r.at[n], where)
        for n, where in enumerate((twin, far, diag))
    ]
    for c in k3:
        c.start()

    for c in halo:
        c.wait_recv()
    widen(mgpad, wide, row, col)
    for g in range(SUB):
        flat[pl.ds(g, PIX, stride=16)] = og[pl.ds(0, PIX), pl.ds(g * LANE, LANE)]

    def line_back(i, _):
        v = row_of_taps(wide, kflat, i, True)
        for j in range(COLS):
            first = flat[pl.ds(pl.multiple_of((i * COLS + j) * 16, 16), SUB)]
            gin[i, j] = (v[j] + first).astype(BF16)
        return 0

    lax.fori_loop(0, ROWS, line_back, 0)

    tok = at_home(part_at, part_xs, part_x, part_ys, part_y)
    lanes = lax.broadcasted_iota(jnp.int32, (SLOT_PAD, 256), 1)
    rows = lax.broadcasted_iota(jnp.int32, (SLOT_PAD, 256), 0)
    named = slots[pl.ds(0, SLOT_PAD), pl.ds(0, 256)].astype(F32)[SLOTS : SLOTS + 1]
    live = jnp.sum(jnp.where(lanes == rows + col * SLOT_PAD, named, 0.0), axis=1, keepdims=True)
    seq[...] = jnp.where(
        live[:SLOTS] > 0.5, tok[:SLOTS].astype(BF16).astype(F32), text[...].astype(F32)
    ).astype(BF16)

    for c in k3:
        c.wait_recv()
    ker_out[col] = (ker_q[0] + ker_q[1] + ker_q[2] + ker_q[3]).astype(BF16)
    k4 = [
        remote(ker_out.at[col], ker_out.at[col], k4_s.at[k], k4_r.at[k], colp[k])
        for k in range(N_COL - 1)
    ]
    for c in k4:
        c.start()
    for k in range(NZ - 1):
        for n, ref in enumerate((gdown, gup)):
            block = ref.at[core, zf[k]]
            remote(block, block, a_s.at[n, k], a_r.at[n, k], zp[k]).wait_recv()
            across(ref, n, k, zf[k], core).start()
    for k in range(N_COL - 1):
        block = ker_out.at[colf[k]]
        remote(block, block, k4_s.at[k], k4_r.at[k], colp[k]).wait_recv()
    for t in range(49):
        kflat[pl.ds(t * 16, SUB)] = ker_out[t // 4, t % 4].astype(F32)
    for g in range(SUB):
        gker[:, g * LANE : (g + 1) * LANE] = kflat[pl.ds(g, 49, stride=16)]
    for n, ref in enumerate((gdown, gup)):
        for k in range(NZ - 1):
            across(ref, n, k, zf[k], 1 - core).wait_recv()
        across(ref, n, NZ - 1, z, 1 - core).wait_recv()
        for k in range(NZ - 1):
            across(ref, n, k, zf[k], core).wait_send()
        across(ref, n, NZ - 1, z, core).wait_send()
    for ref in (g_all, n_all):
        for c in own(*ref):
            c.wait_send()
        for dy in range(1, NY):
            for dx in range(1, NX):
                passed(*ref, dy, dx).wait_send()
    for c in f_halo + list(ng_xs.values()) + list(part_xs.values()) + ng_ys + part_ys + pair:
        c.wait_send()
    for c in z_copies + halo + k1 + h_copies + k2 + a_copies + k3 + k4:
        c.wait_send()


def whole(feat, kern, small, slots, w_up, w_down, text):
    vm = pl.BlockSpec(memory_space=pltpu.VMEM)
    dma = pltpu.SemaphoreType.DMA
    v = pltpu.VMEM
    w = D // NZ // NC
    h = HID // NZ // NC
    band = N_COL * PIX
    every = N_COL * SLOT_PAD
    map_ = (ROWS + 6, COLS + 6, SUB, LANE)
    return pl.pallas_call(
        whole_kernel,
        out_shape=(
            jax.ShapeDtypeStruct((SLOTS, D), BF16),
            jax.ShapeDtypeStruct((ROWS, COLS, SUB, LANE), BF16),
            jax.ShapeDtypeStruct((49, D), F32),
            jax.ShapeDtypeStruct((NC, NZ, w, HID), BF16),
            jax.ShapeDtypeStruct((NC, NZ, h, D), BF16),
        ),
        in_specs=[vm] * 7,
        out_specs=[vm] * 5,
        scratch_shapes=[
            v(map_, BF16), v(map_, F32), v((PIX * 16, LANE), F32), v((49 * 16, LANE), F32),
            v((32, D), F32), v((PIX, D), F32),
            v((N_COL, PIX, D), BF16), v((band, D), BF16), v((every, D), BF16),
            v((band, every), BF16), v((band, D), BF16), v((32, D), F32),
            v((band, HID), F32), v((band, HID), BF16), v((band, HID), BF16),
            v((N_COL, PIX, D), BF16), v((NX - 1, NY, PIX, D), BF16),
            v((NY - 1, PIX, D), BF16), v((NY - 1, PIX, D), BF16),
            v((every, D), BF16), v((NX - 1, NY, SLOT_PAD, D), BF16),
            v((NY - 1, SLOT_PAD, D), BF16), v((NY - 1, SLOT_PAD, D), BF16),
            v((NC, NZ, w, HID), BF16), v((NC, NZ, h, D), BF16),
            v((NZ, w, HID), BF16), v((NZ, h, D), BF16),
            v((NZ - 1, w, HID), BF16), v((NZ - 1, h, D), BF16),
            v((w, HID), BF16), v((h, D), BF16),
            v((NZ, w, HID), BF16), v((NZ, h, D), BF16),
            v((w, HID), BF16), v((h, D), BF16),
            v(map_, BF16), v((ROWS, COLS, SUB, LANE), F32),
            v((16, 4, SUB, LANE), BF16), v((N_COL - 1, 4, SUB, LANE), BF16),
            v((NZ, 4, SUB, LANE), F32), v((4, 4, SUB, LANE), F32), v((16, 4, SUB, LANE), BF16),
            dma((8,)), dma((8,)), dma((NY, NX)), dma((NY, NX)), dma((NY, NX)), dma((NY, NX)),
            dma((NX, NY)), dma((NX, NY)), dma((3,)), dma((3,)),
            dma((NX, NY)), dma((NX, NY)), dma((3,)), dma((3,)),
            dma((8,)), dma((8,)),
            dma((2,)), dma((2,)), dma((2, 7)), dma((2, 7)), dma((2,)), dma((2,)),
            dma((2, 7)), dma((2, 7)), dma((2, 8)), dma((2, 8)),
            dma((15,)), dma((15,)), dma((7,)), dma((7,)), dma((3,)), dma((3,)),
            dma((15,)), dma((15,)),
        ],
        compiler_params=pltpu.CompilerParams(
            collective_id=0, has_side_effects=True, vmem_limit_bytes=VMEM_LIMIT
        ),
    )(feat, kern, small, slots, w_up, w_down, text)


def local(
    features, kernel, ln_gain, ln_bias, w_up, b_up, w_down, layer_scale,
    text_embed, slot_token, seq_grad,
):
    me = lax.axis_index("col")
    feat = features.reshape(ROWS, COLS, SUB, LANE)
    small = jnp.stack([ln_gain, ln_bias, layer_scale, jnp.pad(b_up, (0, D - HID))])
    name = jnp.tile(jnp.pad(slot_token + 1, (0, SLOT_PAD - SLOTS)), N_COL)
    name = jnp.where(lax.iota(jnp.int32, N_COL * SLOT_PAD) // SLOT_PAD == me, name, 0)
    tail = jnp.pad(name.astype(BF16)[None, :], ((0, 3), (0, D - N_COL * SLOT_PAD)))
    slots = jnp.concatenate([seq_grad, tail], axis=0)
    seq, gin, gker, gup, gdown = whole(feat, kernel, small, slots, w_up, w_down, text_embed)
    return (
        seq, gin.reshape(ROWS, COLS, D), gker, gup.reshape(D, HID), gdown.reshape(HID, D),
    )


def solution(mesh):
    placed = (
        P("row", "col", None), P(), P(), P(), P(None, "col"), P("col"), P("col", None), P(),
        P(("row", "col"), None), P(("row", "col")), P(("row", "col"), None),
    )
    return jax.shard_map(
        local,
        mesh=mesh,
        in_specs=placed,
        out_specs=(
            P(("row", "col"), None), P("row", "col", None), P(), P(None, "col"), P("col", None),
        ),
        check_vma=False,
    )
```

time: 165 us -> 118 us (0.72)
  Pallas kernels: 133 us -> 104 us
  matrix products: 9.11 us -> 0 us
  local copies, waits for them, and re-layouts: 17.2 us -> 10.1 us
  other arithmetic: 4.41 us -> 1.56 us
    pallas_call x2 -> x1, Pallas kernels: 133 us -> 104 us  [whole(): pl.pallas_call(whole_kernel, out_shape=(jax.ShapeDtypeStruct((SLOTS, D),...]
    dot_general x9 -> x0, matrix products: 9.11 us -> none  [the longest x1 2 us: local(): part = layer_scale * jnp.dot(pooled, w_down, preferred_element_type=F32)]
    unnamed x50 -> x14, local copies, waits for them, and re-layouts: 10.2 us -> 6.15 us
    reshape x5 -> x0, local copies, waits for them, and re-layouts: 2.84 us -> none  [the longest x2 1.41 us: local(): gain, bias = (ln_gain.reshape(1, D), ln_bias.reshape(1, D))]
where the time goes in v2:
time: 118 us; the launch traced here: 116 us
  Pallas kernels  104 us (88%)
  local copies, waits for them, and re-layouts  10.1 us (9%)
  other arithmetic  1.56 us (1%)
    pallas_call x1, Pallas kernels, whole(): pl.pallas_call(whole_kernel, out_shape=(jax.ShapeDtypeStruct((SLOTS, D),...  104 us
    unnamed x14, local copies, waits for them, and re-layouts  6.15 us

profile of v2, /device:TPU:1, one launch (start us, length us, event | category | flops | bytes accessed | tf_op | source)
XLA Modules:
  0.0 116.3 jit_solution(12825216245509382367)
XLA Ops:
  0.6 0.0 copy-start.4
  0.6 0.0 copy-start.2
  0.7 0.7 broadcast_add_fusion
  1.4 0.0 copy-done.4
  1.4 0.7 stack.16
  2.1 0.7 stack.17
  2.8 0.1 tile.10
  2.9 0.7 pad.12
  3.6 0.8 fusion.1.slots
  4.4 0.9 reshape.73
  5.4 0.0 copy-start.3
  5.4 0.0 copy-done.2
  5.4 0.8 copy-done.3
  6.2 0.0 copy-start
  6.2 1.1 copy-done
  7.3 0.0 copy-start.1
  7.3 1.1 copy-done.1
  8.4 103.9 %shard_map.146 = (bf16[12,1536]{1,0:T(8,128)(2,1)S(1)}, bf16[4,6,12,128]{3,2,1,0:T(8,128)(2,1)S(1)}, f32[49,1536]{1,0:T(8,128)S(1)}, bf16[2,8,96,256]{3,2,1,0:T(8,128)(2,1)S(1)}, bf16[2,8,16,1536]{3,2,1,0:T(8,128)(2,1)S(1)}) custom-call(bf16[4,6,12,128]{3,2,1,0:T(8,128)(2,1)S(1)} %copy.18.feat, f32[49,1536]{1,0:T(8,128)S(1)} %copy-done.2, ...), custom_call_target="tpu_custom_call" | custom-call | tf_op jit(solution)/shard_map/pallas_call | solution.py:525
  112.4 0.1 reshape.77
  112.5 0.7 copy.20
  113.2 0.6 copy.25
  113.8 0.7 copy.26
  114.5 0.9 copy.27
  115.4 0.9 copy.28
  (7 shorter events, 0.1 us)
Async XLA Ops:
  0.6 0.7 copy-start.4
  0.6 4.8 %copy-start.2 = (f32[49,1536]{1,0:T(8,128)S(1)}, f32[49,1536]{1,0:T(8,128)}, u32[]{:S(2)}) copy-start(f32[49,1536]{1,0:T(8,128)} %kern.1) | copy-start | bytes 903172
  5.4 0.8 copy-start.3
  6.2 1.1 copy-start
  7.3 1.1 copy-start.1

commit v3 on v2

--- a/solution.py
+++ b/solution.py
@@ -31,7 +31,7 @@
     barrier = pltpu.get_barrier_semaphore()
     for device in where:
         pl.semaphore_signal(barrier, inc=1, device_id=device, device_id_type=MESH)
-    pl.semaphore_wait(barrier, len(where))
+    return barrier
 
 
 def halo_copies(pad, row, col, send, recv):
@@ -84,14 +84,18 @@
 
 
 def whole_kernel(
-    feat, kern, small, slots, w_up, w_down, text,
+    feat, kern, ln_gain, ln_bias, b_up, layer_scale, slot, seq_grad, w_up_hbm, w_down_hbm, text_hbm,
     seq, gin, gker, gup, gdown,
+    w_up, w_down, text, block,
     pad, wide, flat, kflat, feat2, mixed, normed, band, every, select, bg, og, act_grad,
     act, pre_grad, ng, ng_x, ng_t, ng_y, part, part_x, part_t, part_y,
-    up, down, up0, down0, up1, down1, up2, down2, up_h, down_h, up_c, down_c,
-    mgpad, mwide, ker, ker_in, ker_z, ker_q, ker_out,
-    f_s, f_r, n_s, n_r, g_s, g_r, nx_s, nx_r, ny_s, ny_r, px_s, px_r, py_s, py_r, halo_s, halo_r,
-    c_s, c_r, z_s, z_r, h_s, h_r, a_s, a_r, b_s, b_r, k1_s, k1_r, k2_s, k2_r, k3_s, k3_r, k4_s, k4_r,
+    up, down, up0, down0, up1, down1, up2, down2, up_h, down_h, up_q, down_c,
+    mgpad, mwide, ker, ker_p, ker_h, ker_in, ker_z, ker_z_in, ker_out,
+    w_s, f_s, f_r, n_s, n_r, g_s, g_r,
+    nx_s, nx_r, ny_s, ny_r, px_s, px_r, py_s, py_r, halo_s, halo_r,
+    c_s, c_r, dz_s, dz_r, uz_s, uz_r, h_s, h_r,
+    da_s, da_r, ua_s, ua_r, uf_s, uf_r, dt_s, dt_r, ut_s, ut_r,
+    k0_s, k0_r, k1_s, k1_r, k2_s, k2_r, k4_s, k4_r, k5_s, k5_r,
 ):
     row, col = lax.axis_index("row"), lax.axis_index("col")
     y, x = col // NX, lax.rem(col, NX)
@@ -110,15 +114,71 @@
     zp = [at(yh, k, core) for k in zb]
     twin = at(yh, z, 1 - core)
     far = at(1 - yh, z, core)
-    diag = at(1 - yh, z, 1 - core)
+    rowp = zp + [at(1 - yh, lax.rem(z + k, NZ), core) for k in range(NZ)]
     around = [
         (lax.rem(row + a + N_ROW, N_ROW), lax.rem(col + b + N_COL, N_COL)) for a, b in DIRS
     ]
-    gain, bias, scale = small[0:1], small[1:2], small[2:3]
+    fetch = [
+        pltpu.make_async_copy(a, b, w_s.at[k])
+        for k, (a, b) in enumerate(((w_up_hbm, w_up), (w_down_hbm, w_down), (text_hbm, text)))
+    ]
+    for c in fetch:
+        c.start()
+    gain, bias = ln_gain[...].reshape(1, D), ln_bias[...].reshape(1, D)
+    b_row = b_up[...].reshape(1, HID)
     slot_rows = lambda d: pl.ds(pl.multiple_of(d * SLOT_PAD, SLOT_PAD), SLOT_PAD)
 
+    partners = around + colp + rowp + [twin]
+    barrier = greet(partners)
     pad[pl.ds(3, ROWS), pl.ds(3, COLS)] = feat[...]
-    every[slot_rows(col)] = slots[...]
+    lane = lax.broadcasted_iota(jnp.int32, (1, 256), 1)
+    name = jnp.zeros((1, 256), jnp.int32)
+    for r in range(SLOTS):
+        name = jnp.where(lane == col * SLOT_PAD + r, slot[r] + 1, name)
+    block[...] = jnp.zeros_like(block)
+    block[pl.ds(0, SLOTS)] = seq_grad[...].astype(F32)
+    block[pl.ds(SLOTS, 1), pl.ds(0, 256)] = name.astype(F32)
+    every[slot_rows(col)] = block[...].astype(BF16)
+    pl.semaphore_wait(barrier, len(partners))
+
+    f_halo = halo_copies(pad, row, col, f_s, f_r)
+    for c in f_halo:
+        c.start()
+
+    n_at = lambda d: normed.at[d]
+    g_at = lambda d: every.at[slot_rows(d)]
+
+    def own(at_, send, recv):
+        out = []
+        for dy in range(1, NY):
+            out.append(remote(at_(col), at_(col), send.at[dy, 0], recv.at[dy, 0], yp[dy - 1]))
+        for dx in range(1, NX):
+            out.append(remote(at_(col), at_(col), send.at[0, dx], recv.at[0, dx], xp[dx - 1]))
+        return out
+
+    def passed(at_, send, recv, dy, dx):
+        b = peer(-dy, 0)
+        return remote(at_(b), at_(b), send.at[dy, dx], recv.at[dy, dx], xp[dx - 1])
+
+    def came(at_, send, recv, dy, dx):
+        b = peer(-dy, -dx)
+        return remote(at_(b), at_(b), send.at[dy, dx], recv.at[dy, dx], (row, peer(dy, dx)))
+
+    g_all, n_all = (g_at, g_s, g_r), (n_at, n_s, n_r)
+
+    def onward(ref):
+        for a in range(1, 4):
+            came(*ref, a, 0).wait_recv()
+            for b in range(1, 4):
+                passed(*ref, a, b).start()
+
+    def arrived(ref):
+        for a in range(4):
+            for b in range(1, 4):
+                came(*ref, a, b).wait_recv()
+
+    for c in own(*g_all):
+        c.start()
     for g in range(SUB):
         kflat[pl.ds(g, 49, stride=16)] = kern[:, g * LANE : (g + 1) * LANE]
     for i in range(ROWS):
@@ -127,46 +187,6 @@
     feat2[...] = jnp.zeros_like(feat2)
     for g in range(SUB):
         feat2[pl.ds(0, PIX), pl.ds(g * LANE, LANE)] = flat[pl.ds(g, PIX, stride=16)]
-    greet(around + colp + zp + [twin, far, diag])
-
-    f_halo = halo_copies(pad, row, col, f_s, f_r)
-    for c in f_halo:
-        c.start()
-
-    n_at = lambda d: normed.at[d]
-    g_at = lambda d: every.at[slot_rows(d)]
-
-    def own(at_, send, recv):
-        out = []
-        for dy in range(1, NY):
-            out.append(remote(at_(col), at_(col), send.at[dy, 0], recv.at[dy, 0], yp[dy - 1]))
-        for dx in range(1, NX):
-            out.append(remote(at_(col), at_(col), send.at[0, dx], recv.at[0, dx], xp[dx - 1]))
-        return out
-
-    def passed(at_, send, recv, dy, dx):
-        b = peer(-dy, 0)
-        return remote(at_(b), at_(b), send.at[dy, dx], recv.at[dy, dx], xp[dx - 1])
-
-    def came(at_, send, recv, dy, dx):
-        b = peer(-dy, -dx)
-        return remote(at_(b), at_(b), send.at[dy, dx], recv.at[dy, dx], (row, peer(dy, dx)))
-
-    g_all, n_all = (g_at, g_s, g_r), (n_at, n_s, n_r)
-
-    def onward(ref):
-        for dy in range(1, NY):
-            came(*ref, dy, 0).wait_recv()
-            for dx in range(1, NX):
-                passed(*ref, dy, dx).start()
-
-    def arrived(ref):
-        for dx in range(1, NX):
-            for dy in range(NY):
-                came(*ref, dy, dx).wait_recv()
-
-    for c in own(*g_all):
-        c.start()
     for c in f_halo:
         c.wait_recv()
     onward(g_all)
@@ -190,6 +210,7 @@
     onward(n_all)
 
     arrived(g_all)
+    slots_row = name.astype(F32)
     names = jnp.zeros((SLOT_PAD, 256), F32)
     for d in range(N_COL):
         names = names + every[pl.ds(d * SLOT_PAD, SLOT_PAD), pl.ds(0, 256)].astype(F32)
@@ -215,10 +236,12 @@
     def grads(c, _):
         cut = pl.ds(pl.multiple_of(c * 512, 512), 512)
         g = dot(select[...], every[:, cut], 1, 0) * 0.25
-        bg[:, cut] = (g * small[2:3, cut]).astype(BF16)
+        bg[:, cut] = (g * layer_scale[cut].reshape(1, 512)).astype(BF16)
         og[:, cut] = dot(mine, every[:, cut], 1, 0) * 0.25
         return 0
 
+    for c in fetch:
+        c.wait()
     lax.fori_loop(0, 3, grads, 0)
 
     def hidden_grads(r, _):
@@ -235,7 +258,7 @@
 
     def hidden(r, _):
         cut = pl.ds(pl.multiple_of(r * 128, 128), 128)
-        v = dot(band[cut], w_up[...], 1, 0) + small[3:4, 0:HID]
+        v = dot(band[cut], w_up[...], 1, 0) + b_row
         k0, k1 = 0.7978845608028654, 0.044715
         t = jnp.tanh(k0 * (v + k1 * v * v * v))
         act[cut] = (0.5 * v * (1.0 + t)).astype(BF16)
@@ -308,16 +331,15 @@
     pair[0].start()
     for c in range(4):
         v = dot(band[:, c * 384 : (c + 1) * 384], pre_grad[...], 0, 0)
-        for k in range(4):
-            b = c * 4 + k
-            up[b // NZ, b % NZ] = v[k * 96 : (k + 1) * 96].astype(BF16)
+        for k in range(8):
+            up[c // 2, c % 2, k] = v[k * 48 : (k + 1) * 48].astype(BF16)
     pair[1].start()
 
     pooled = (dot(select[...], act[...], 0, 0) * 0.25).astype(BF16)
 
     def tokens(c, _):
         cut = pl.ds(pl.multiple_of(c * 512, 512), 512)
-        v = dot(pooled, w_down[:, cut], 1, 0) * small[2:3, cut]
+        v = dot(pooled, w_down[:, cut], 1, 0) * layer_scale[cut].reshape(1, 512)
         v = v + 0.25 * dot(mine, feat2[:, cut].astype(BF16), 0, 0)
         part[:, cut] = v.astype(BF16)
         return 0
@@ -332,14 +354,14 @@
         c.wait_recv()
     for k in range(NZ):
         down_h[k] = (down[core, k].astype(F32) + down0[k].astype(F32)).astype(BF16)
-        up_h[k] = (up[core, k].astype(F32) + up0[k].astype(F32)).astype(BF16)
-    z_copies = []
-    for k in range(NZ - 1):
-        z_copies.append(
-            remote(down_h.at[zb[k]], down1.at[k], z_s.at[0, k], z_r.at[0, k], zp[k])
-        )
-        z_copies.append(remote(up_h.at[zb[k]], up1.at[k], z_s.at[1, k], z_r.at[1, k], zp[k]))
-    for c in z_copies:
+        for n in range(2):
+            up_h[n, k] = (up[core, n, k].astype(F32) + up0[n, k].astype(F32)).astype(BF16)
+    up_far = remote(up_h.at[1 - yh], up1, h_s.at[0], h_r.at[0], far)
+    up_far.start()
+    down_z = [
+        remote(down_h.at[zb[k]], down1.at[k], dz_s.at[k], dz_r.at[k], zp[k]) for k in range(NZ - 1)
+    ]
+    for c in down_z:
         c.start()
 
     ng_ys = along_y(ng_at, ng_xs, ng_x, ng_t, ng_y, ny_s, ny_r)
@@ -375,78 +397,55 @@
                 acc[q] = acc[q] + jnp.sum(line[q : q + COLS] * own_line, axis=0)
         for q in range(7):
             t = p * 7 + q
-            ker[t // 4, lax.rem(t, 4)] = acc[q].astype(BF16)
+            ker[lax.rem(t, 2), t // 4, lax.rem(t // 2, 2)] = acc[q].astype(BF16)
         return 0
 
     lax.fori_loop(0, 7, taps, 0)
     for t in range(49, 64):
-        ker[t // 4, t % 4] = jnp.zeros((SUB, LANE), BF16)
+        ker[t % 2, t // 4, t // 2 % 2] = jnp.zeros((SUB, LANE), BF16)
+    k0 = remote(ker.at[1 - core], ker_p, k0_s.at[0], k0_r.at[0], twin)
+    k0.start()
+
+    k0.wait_recv()
+    for k in range(16):
+        ker_h[k] = (ker[core, k].astype(F32) + ker_p[k].astype(F32)).astype(BF16)
     k1 = [
-        remote(ker.at[colb[k]], ker_in.at[k], k1_s.at[k], k1_r.at[k], colp[k])
+        remote(ker_h.at[colb[k]], ker_in.at[k], k1_s.at[k], k1_r.at[k], colp[k])
         for k in range(N_COL - 1)
     ]
     for c in k1:
         c.start()
+    for c in down_z:
+        c.wait_recv()
+    v = down_h[z].astype(F32)
+    for k in range(NZ - 1):
+        v = v + down1[k].astype(F32)
+    down_c[...] = v.astype(BF16)
+    down_far = remote(down_c, down2, h_s.at[1], h_r.at[1], far)
+    down_far.start()
+    up_far.wait_recv()
+    for k in range(NZ):
+        up_q[k] = (up_h[yh, k].astype(F32) + up1[k].astype(F32)).astype(BF16)
+    up_z = [
+        remote(up_q.at[zb[k]], up2.at[k], uz_s.at[k], uz_r.at[k], zp[k]) for k in range(NZ - 1)
+    ]
+    for c in up_z:
+        c.start()
+
     part_ys = along_y(part_at, part_xs, part_x, part_t, part_y, py_s, py_r)
-
-    for c in z_copies:
-        c.wait_recv()
-    ds, us = down_h[z].astype(F32), up_h[z].astype(F32)
-    for k in range(NZ - 1):
-        ds = ds + down1[k].astype(F32)
-        us = us + up1[k].astype(F32)
-    down_c[...] = ds.astype(BF16)
-    up_c[...] = us.astype(BF16)
-    h_copies = [
-        remote(down_c, down2, h_s.at[0], h_r.at[0], far),
-        remote(up_c, up2, h_s.at[1], h_r.at[1], far),
-    ]
-    for c in h_copies:
-        c.start()
 
     for c in k1:
         c.wait_recv()
-    ks = ker[col].astype(F32)
+    v = ker_h[col].astype(F32)
     for k in range(N_COL - 1):
-        ks = ks + ker_in[k].astype(F32)
-    ker_z[z] = ks
+        v = v + ker_in[k].astype(F32)
+    ker_z[...] = v.astype(BF16)
+    place = yh * NZ + z
+    ker_z_in[place] = ker_z[...]
     k2 = [
-        remote(ker_z.at[z], ker_z.at[z], k2_s.at[k], k2_r.at[k], zp[k]) for k in range(NZ - 1)
+        remote(ker_z, ker_z_in.at[place], k2_s.at[k], k2_r.at[k], rowp[k]) for k in range(15)
     ]
     for c in k2:
-        c.start()
-
-    for c in h_copies:
-        c.wait_recv()
-    gdown[core, z] = (down_c[...].astype(F32) + down2[...].astype(F32)).astype(BF16)
-    gup[core, z] = (up_c[...].astype(F32) + up2[...].astype(F32)).astype(BF16)
-    a_copies = []
-    for k in range(NZ - 1):
-        a_copies.append(
-            remote(gdown.at[core, z], gdown.at[core, z], a_s.at[0, k], a_r.at[0, k], zp[k])
-        )
-        a_copies.append(remote(gup.at[core, z], gup.at[core, z], a_s.at[1, k], a_r.at[1, k], zp[k]))
-    for c in a_copies:
-        c.start()
-
-    def across(ref, n, k, zz, cc):
-        return remote(ref.at[cc, zz], ref.at[cc, zz], b_s.at[n, k], b_r.at[n, k], twin)
-
-    across(gdown, 0, NZ - 1, z, core).start()
-    across(gup, 1, NZ - 1, z, core).start()
-
-    for c in k2:
-        c.wait_recv()
-    ks = ker_z[0]
-    for k in range(1, NZ):
-        ks = ks + ker_z[k]
-    q = yh * NC + core
-    ker_q[q] = ks
-    k3 = [
-        remote(ker_q.at[q], ker_q.at[q], k3_s.at[n], k3_r.at[n], where)
-        for n, where in enumerate((twin, far, diag))
-    ]
-    for c in k3:
         c.start()
 
     for c in halo:
@@ -464,43 +463,91 @@
 
     lax.fori_loop(0, ROWS, line_back, 0)
 
+    for c in up_z:
+        c.wait_recv()
+    v = up_q[z].astype(F32)
+    for k in range(NZ - 1):
+        v = v + up2[k].astype(F32)
+    gup[core, yh, z] = v.astype(BF16)
+
+    def up_to(where, cc, hh, zz, send, recv):
+        ref = gup.at[cc, hh, zz]
+        return remote(ref, ref, send, recv, where)
+
+    def up_home(k):
+        return lax.rem(z - k + NZ, NZ)
+
+    ua = [up_to(zp[k], core, yh, z, ua_s.at[k], ua_r.at[k]) for k in range(NZ - 1)]
+    uf = [up_to(far, core, yh, up_home(k), uf_s.at[k], uf_r.at[k]) for k in range(NZ)]
+    ut = [up_to(twin, core, yh, up_home(k), ut_s.at[0, k], ut_r.at[0, k]) for k in range(NZ)]
+    vt = [up_to(twin, core, 1 - yh, up_home(k), ut_s.at[1, k], ut_r.at[1, k]) for k in range(NZ)]
+    for c in ua:
+        c.start()
+    uf[0].start()
+    ut[0].start()
+    down_far.wait_recv()
+    gdown[core, z] = (down_c[...].astype(F32) + down2[...].astype(F32)).astype(BF16)
+
+    def down_to(where, cc, zz, send, recv):
+        ref = gdown.at[cc, zz]
+        return remote(ref, ref, send, recv, where)
+
+    da = [down_to(zp[k], core, z, da_s.at[k], da_r.at[k]) for k in range(NZ - 1)]
+    dt = [down_to(twin, core, up_home(k), dt_s.at[k], dt_r.at[k]) for k in range(NZ)]
+    for c in da:
+        c.start()
+    dt[0].start()
+
+    for k in range(15):
+        k2[k].wait_recv()
+    v = ker_z_in[0].astype(F32)
+    for k in range(1, 16):
+        v = v + ker_z_in[k].astype(F32)
+    ker_out[core, col] = v.astype(BF16)
+    k4 = [
+        remote(ker_out.at[core, col], ker_out.at[core, col], k4_s.at[k], k4_r.at[k], colp[k])
+        for k in range(N_COL - 1)
+    ]
+    for c in k4:
+        c.start()
+
     tok = at_home(part_at, part_xs, part_x, part_ys, part_y)
     lanes = lax.broadcasted_iota(jnp.int32, (SLOT_PAD, 256), 1)
     rows = lax.broadcasted_iota(jnp.int32, (SLOT_PAD, 256), 0)
-    named = slots[pl.ds(0, SLOT_PAD), pl.ds(0, 256)].astype(F32)[SLOTS : SLOTS + 1]
+    named = slots_row
     live = jnp.sum(jnp.where(lanes == rows + col * SLOT_PAD, named, 0.0), axis=1, keepdims=True)
     seq[...] = jnp.where(
         live[:SLOTS] > 0.5, tok[:SLOTS].astype(BF16).astype(F32), text[...].astype(F32)
     ).astype(BF16)
 
-    for c in k3:
-        c.wait_recv()
-    ker_out[col] = (ker_q[0] + ker_q[1] + ker_q[2] + ker_q[3]).astype(BF16)
-    k4 = [
-        remote(ker_out.at[col], ker_out.at[col], k4_s.at[k], k4_r.at[k], colp[k])
-        for k in range(N_COL - 1)
-    ]
-    for c in k4:
-        c.start()
-    for k in range(NZ - 1):
-        for n, ref in enumerate((gdown, gup)):
-            block = ref.at[core, zf[k]]
-            remote(block, block, a_s.at[n, k], a_r.at[n, k], zp[k]).wait_recv()
-            across(ref, n, k, zf[k], core).start()
+    for k in range(1, NZ):
+        b = up_home(k)
+        up_to(zp[k - 1], core, yh, b, ua_s.at[k - 1], ua_r.at[k - 1]).wait_recv()
+        uf[k].start()
+        ut[k].start()
     for k in range(N_COL - 1):
-        block = ker_out.at[colf[k]]
-        remote(block, block, k4_s.at[k], k4_r.at[k], colp[k]).wait_recv()
+        b = ker_out.at[core, colf[k]]
+        remote(b, b, k4_s.at[k], k4_r.at[k], colp[k]).wait_recv()
+    k5 = remote(ker_out.at[core], ker_out.at[core], k5_s.at[0], k5_r.at[0], twin)
+    k5.start()
+    for k in range(1, NZ):
+        b = up_home(k)
+        down_to(zp[k - 1], core, b, da_s.at[k - 1], da_r.at[k - 1]).wait_recv()
+        dt[k].start()
+    b = ker_out.at[1 - core]
+    remote(b, b, k5_s.at[0], k5_r.at[0], twin).wait_recv()
     for t in range(49):
-        kflat[pl.ds(t * 16, SUB)] = ker_out[t // 4, t % 4].astype(F32)
+        kflat[pl.ds(t * 16, SUB)] = ker_out[t % 2, t // 4, t // 2 % 2].astype(F32)
     for g in range(SUB):
         gker[:, g * LANE : (g + 1) * LANE] = kflat[pl.ds(g, 49, stride=16)]
-    for n, ref in enumerate((gdown, gup)):
-        for k in range(NZ - 1):
-            across(ref, n, k, zf[k], 1 - core).wait_recv()
-        across(ref, n, NZ - 1, z, 1 - core).wait_recv()
-        for k in range(NZ - 1):
-            across(ref, n, k, zf[k], core).wait_send()
-        across(ref, n, NZ - 1, z, core).wait_send()
+    for k in range(NZ):
+        up_to(far, core, 1 - yh, up_home(k), uf_s.at[k], uf_r.at[k]).wait_recv()
+        vt[k].start()
+    for k in range(NZ):
+        b = up_home(k)
+        up_to(twin, 1 - core, yh, b, ut_s.at[0, k], ut_r.at[0, k]).wait_recv()
+        up_to(twin, 1 - core, 1 - yh, b, ut_s.at[1, k], ut_r.at[1, k]).wait_recv()
+        down_to(twin, 1 - core, b, dt_s.at[k], dt_r.at[k]).wait_recv()
     for ref in (g_all, n_all):
         for c in own(*ref):
             c.wait_send()
@@ -509,15 +556,17 @@
                 passed(*ref, dy, dx).wait_send()
     for c in f_halo + list(ng_xs.values()) + list(part_xs.values()) + ng_ys + part_ys + pair:
         c.wait_send()
-    for c in z_copies + halo + k1 + h_copies + k2 + a_copies + k3 + k4:
+    for c in halo + [up_far, down_far, k0, k5] + down_z + up_z + k1 + k2 + k4:
         c.wait_send()
-
-
-def whole(feat, kern, small, slots, w_up, w_down, text):
+    for c in ua + uf + ut + vt + da + dt:
+        c.wait_send()
+
+
+def whole(*operands):
     vm = pl.BlockSpec(memory_space=pltpu.VMEM)
     dma = pltpu.SemaphoreType.DMA
     v = pltpu.VMEM
-    w = D // NZ // NC
+    w = D // NZ // NC // 2
     h = HID // NZ // NC
     band = N_COL * PIX
     every = N_COL * SLOT_PAD
@@ -528,12 +577,15 @@
             jax.ShapeDtypeStruct((SLOTS, D), BF16),
             jax.ShapeDtypeStruct((ROWS, COLS, SUB, LANE), BF16),
             jax.ShapeDtypeStruct((49, D), F32),
-            jax.ShapeDtypeStruct((NC, NZ, w, HID), BF16),
+            jax.ShapeDtypeStruct((NC, 2, NZ, w, HID), BF16),
             jax.ShapeDtypeStruct((NC, NZ, h, D), BF16),
         ),
-        in_specs=[vm] * 7,
+        in_specs=[vm] * 6
+        + [pl.BlockSpec(memory_space=pltpu.SMEM), vm]
+        + [pl.BlockSpec(memory_space=pl.ANY)] * 3,
         out_specs=[vm] * 5,
         scratch_shapes=[
+            v((D, HID), BF16), v((HID, D), BF16), v((SLOTS, D), BF16), v((SLOT_PAD, D), F32),
             v(map_, BF16), v(map_, F32), v((PIX * 16, LANE), F32), v((49 * 16, LANE), F32),
             v((32, D), F32), v((PIX, D), F32),
             v((N_COL, PIX, D), BF16), v((band, D), BF16), v((every, D), BF16),
@@ -543,42 +595,42 @@
             v((NY - 1, PIX, D), BF16), v((NY - 1, PIX, D), BF16),
             v((every, D), BF16), v((NX - 1, NY, SLOT_PAD, D), BF16),
             v((NY - 1, SLOT_PAD, D), BF16), v((NY - 1, SLOT_PAD, D), BF16),
-            v((NC, NZ, w, HID), BF16), v((NC, NZ, h, D), BF16),
-            v((NZ, w, HID), BF16), v((NZ, h, D), BF16),
-            v((NZ - 1, w, HID), BF16), v((NZ - 1, h, D), BF16),
-            v((w, HID), BF16), v((h, D), BF16),
-            v((NZ, w, HID), BF16), v((NZ, h, D), BF16),
-            v((w, HID), BF16), v((h, D), BF16),
+            v((NC, 2, NZ, w, HID), BF16), v((NC, NZ, h, D), BF16),
+            v((2, NZ, w, HID), BF16), v((NZ, h, D), BF16),
+            v((NZ, w, HID), BF16), v((NZ - 1, h, D), BF16),
+            v((NZ - 1, w, HID), BF16), v((h, D), BF16),
+            v((2, NZ, w, HID), BF16), v((NZ, h, D), BF16),
+            v((NZ, w, HID), BF16), v((h, D), BF16),
             v(map_, BF16), v((ROWS, COLS, SUB, LANE), F32),
-            v((16, 4, SUB, LANE), BF16), v((N_COL - 1, 4, SUB, LANE), BF16),
-            v((NZ, 4, SUB, LANE), F32), v((4, 4, SUB, LANE), F32), v((16, 4, SUB, LANE), BF16),
-            dma((8,)), dma((8,)), dma((NY, NX)), dma((NY, NX)), dma((NY, NX)), dma((NY, NX)),
+            v((NC, 16, 2, SUB, LANE), BF16), v((16, 2, SUB, LANE), BF16),
+            v((16, 2, SUB, LANE), BF16), v((15, 2, SUB, LANE), BF16),
+            v((2, SUB, LANE), BF16), v((16, 2, SUB, LANE), BF16), v((NC, 16, 2, SUB, LANE), BF16),
+            dma((3,)), dma((8,)), dma((8,)),
+            dma((NY, NX)), dma((NY, NX)), dma((NY, NX)), dma((NY, NX)),
             dma((NX, NY)), dma((NX, NY)), dma((3,)), dma((3,)),
             dma((NX, NY)), dma((NX, NY)), dma((3,)), dma((3,)),
             dma((8,)), dma((8,)),
-            dma((2,)), dma((2,)), dma((2, 7)), dma((2, 7)), dma((2,)), dma((2,)),
-            dma((2, 7)), dma((2, 7)), dma((2, 8)), dma((2, 8)),
-            dma((15,)), dma((15,)), dma((7,)), dma((7,)), dma((3,)), dma((3,)),
-            dma((15,)), dma((15,)),
+            dma((2,)), dma((2,)), dma((7,)), dma((7,)), dma((7,)), dma((7,)), dma((2,)), dma((2,)),
+            dma((7,)), dma((7,)), dma((7,)), dma((7,)), dma((8,)), dma((8,)), dma((8,)), dma((8,)),
+            dma((2, 8)), dma((2, 8)),
+            dma((1,)), dma((1,)), dma((15,)), dma((15,)), dma((15,)), dma((15,)),
+            dma((15,)), dma((15,)), dma((1,)), dma((1,)),
         ],
         compiler_params=pltpu.CompilerParams(
             collective_id=0, has_side_effects=True, vmem_limit_bytes=VMEM_LIMIT
         ),
-    )(feat, kern, small, slots, w_up, w_down, text)
+    )(*operands)
 
 
 def local(
     features, kernel, ln_gain, ln_bias, w_up, b_up, w_down, layer_scale,
     text_embed, slot_token, seq_grad,
 ):
-    me = lax.axis_index("col")
     feat = features.reshape(ROWS, COLS, SUB, LANE)
-    small = jnp.stack([ln_gain, ln_bias, layer_scale, jnp.pad(b_up, (0, D - HID))])
-    name = jnp.tile(jnp.pad(slot_token + 1, (0, SLOT_PAD - SLOTS)), N_COL)
-    name = jnp.where(lax.iota(jnp.int32, N_COL * SLOT_PAD) // SLOT_PAD == me, name, 0)
-    tail = jnp.pad(name.astype(BF16)[None, :], ((0, 3), (0, D - N_COL * SLOT_PAD)))
-    slots = jnp.concatenate([seq_grad, tail], axis=0)
-    seq, gin, gker, gup, gdown = whole(feat, kernel, small, slots, w_up, w_down, text_embed)
+    seq, gin, gker, gup, gdown = whole(
+        feat, kernel, ln_gain, ln_bias, b_up, layer_scale, slot_token, seq_grad, w_up, w_down,
+        text_embed,
+    )
     return (
         seq, gin.reshape(ROWS, COLS, D), gker, gup.reshape(D, HID), gdown.reshape(HID, D),
     )

time: 118 us -> 118 us (level)
  other arithmetic: 1.56 us -> 0 us
    unnamed x14 -> x24, local copies, waits for them, and re-layouts: 6.15 us -> 8.99 us
    another operation x6 -> x0, local copies, waits for them, and re-layouts: 1.5 us -> none  [the longest x4 1.42 us: local(): jnp.stack([ln_gain, ln_bias, layer_scale, jnp.pad(b_up, (0, D - HID))])]
where the time goes in v3:
time: 118 us; the launch traced here: 116 us
  Pallas kernels  105 us (89%)
  local copies, waits for them, and re-layouts  10.8 us (9%)
    pallas_call x1, Pallas kernels, whole(): pl.pallas_call(whole_kernel, out_shape=(jax.ShapeDtypeStruct((SLOTS, D),...  105 us
    unnamed x24, local copies, waits for them, and re-layouts  8.99 us

profile of v3, /device:TPU:1, one launch (start us, length us, event | category | flops | bytes accessed | tf_op | source)
XLA Modules:
  0.0 116.5 jit_solution(12136982428036332030)
XLA Ops:
  0.6 0.0 copy-start.2
  0.6 1.0 reshape.22
  1.6 0.0 copy-start.5
  1.6 0.0 copy-start.6
  1.7 0.0 copy-start.7
  1.7 0.0 copy-done.2
  1.7 0.6 copy-done.5
  2.3 0.0 copy-done.6
  2.3 0.0 copy-done.7
  2.4 0.0 copy-start
  2.4 1.1 copy-done
  3.5 0.0 copy-start.1
  3.5 1.1 copy-done.1
  4.6 0.8 copy-done.3
  5.4 0.8 copy-done.4
  6.2 0.7 copy-done.8
  6.9 0.7 copy-done.9
  7.6 105.0 %shard_map.146 = (bf16[12,1536]{1,0:T(8,128)(2,1)S(1)}, bf16[4,6,12,128]{3,2,1,0:T(8,128)(2,1)S(1)}, f32[49,1536]{1,0:T(8,128)S(1)}, bf16[2,2,8,48,256]{4,3,2,1,0:T(8,128)(2,1)S(1)}, bf16[2,8,16,1536]{3,2,1,0:T(8,128)(2,1)S(1)}) custom-call(bf16[4,6,12,128]{3,2,1,0:T(8,128)(2,1)S(1)} %copy.18.feat, f32[49,1536]{1,0:T(8,128)S(1)} %copy-done.2, ...), custom_call_target="tpu_custom_call" | custom-call | tf_op jit(solution)/shard_map/pallas_call | solution.py:574
  112.6 0.1 reshape.26
  112.7 0.7 copy.20
  113.3 0.6 copy.25
  114.0 0.7 copy.26
  114.7 0.9 copy.27
  115.6 0.9 copy.28
  (5 shorter events, 0.0 us)
Async XLA Ops:
  0.6 1.1 copy-start.2
  1.6 0.7 copy-start.5
  1.6 0.7 copy-start.6
  1.7 0.7 copy-start.7
  2.4 1.1 copy-start
  3.5 1.1 copy-start.1
  4.6 0.8 copy-start.3
  5.4 0.8 copy-start.4
  6.2 0.7 copy-start.8
  6.9 0.7 copy-start.9

commit v4 on v3

--- a/solution.py
+++ b/solution.py
@@ -14,7 +14,7 @@
 HID = 256
 DIRS = [(a, b) for a in (-1, 0, 1) for b in (-1, 0, 1) if (a, b) != (0, 0)]
 MESH = pl.DeviceIdType.MESH
-VMEM_LIMIT = 48 * 1024 * 1024
+VMEM_LIMIT = 52000 * 1024
 SRC_ROW = {1: (1, 3), 0: (0, 4), -1: (0, 3)}
 DST_ROW = {1: 0, 0: 3, -1: 7}
 SRC_COL = {1: (3, 3), 0: (0, 6), -1: (0, 3)}
@@ -84,9 +84,10 @@
 
 
 def whole_kernel(
-    feat, kern, ln_gain, ln_bias, b_up, layer_scale, slot, seq_grad, w_up_hbm, w_down_hbm, text_hbm,
+    feat, slot, seq_grad_hbm, kern_hbm, ln_gain_hbm, ln_bias_hbm, b_up_hbm, layer_scale_hbm,
+    w_down_hbm, w_up_hbm, text_hbm,
     seq, gin, gker, gup, gdown,
-    w_up, w_down, text, block,
+    seq_grad, kern, ln_gain, ln_bias, b_up, layer_scale, w_down, w_up, text, block,
     pad, wide, flat, kflat, feat2, mixed, normed, band, every, select, bg, og, act_grad,
     act, pre_grad, ng, ng_x, ng_t, ng_y, part, part_x, part_t, part_y,
     up, down, up0, down0, up1, down1, up2, down2, up_h, down_h, up_q, down_c,
@@ -118,14 +119,16 @@
     around = [
         (lax.rem(row + a + N_ROW, N_ROW), lax.rem(col + b + N_COL, N_COL)) for a, b in DIRS
     ]
+    held_in = (seq_grad, kern, ln_gain, ln_bias, b_up, layer_scale, w_down, w_up, text)
+    from_hbm = (
+        seq_grad_hbm, kern_hbm, ln_gain_hbm, ln_bias_hbm, b_up_hbm, layer_scale_hbm,
+        w_down_hbm, w_up_hbm, text_hbm,
+    )
     fetch = [
-        pltpu.make_async_copy(a, b, w_s.at[k])
-        for k, (a, b) in enumerate(((w_up_hbm, w_up), (w_down_hbm, w_down), (text_hbm, text)))
+        pltpu.make_async_copy(a, b, w_s.at[k]) for k, (a, b) in enumerate(zip(from_hbm, held_in))
     ]
     for c in fetch:
         c.start()
-    gain, bias = ln_gain[...].reshape(1, D), ln_bias[...].reshape(1, D)
-    b_row = b_up[...].reshape(1, HID)
     slot_rows = lambda d: pl.ds(pl.multiple_of(d * SLOT_PAD, SLOT_PAD), SLOT_PAD)
 
     partners = around + colp + rowp + [twin]
@@ -136,6 +139,7 @@
     for r in range(SLOTS):
         name = jnp.where(lane == col * SLOT_PAD + r, slot[r] + 1, name)
     block[...] = jnp.zeros_like(block)
+    fetch[0].wait()
     block[pl.ds(0, SLOTS)] = seq_grad[...].astype(F32)
     block[pl.ds(SLOTS, 1), pl.ds(0, 256)] = name.astype(F32)
     every[slot_rows(col)] = block[...].astype(BF16)
@@ -179,6 +183,10 @@
 
     for c in own(*g_all):
         c.start()
+    for c in fetch[1:6]:
+        c.wait()
+    gain, bias = ln_gain[...].reshape(1, D), ln_bias[...].reshape(1, D)
+    b_row = b_up[...].reshape(1, HID)
     for g in range(SUB):
         kflat[pl.ds(g, 49, stride=16)] = kern[:, g * LANE : (g + 1) * LANE]
     for i in range(ROWS):
@@ -240,7 +248,7 @@
         og[:, cut] = dot(mine, every[:, cut], 1, 0) * 0.25
         return 0
 
-    for c in fetch:
+    for c in fetch[6:]:
         c.wait()
     lax.fori_loop(0, 3, grads, 0)
 
@@ -347,8 +355,6 @@
     lax.fori_loop(0, 3, tokens, 0)
     part_at = lambda d: part.at[slot_rows(d)]
     part_xs = across_x(part_at, part_x, px_s, px_r)
-    for c in part_xs.values():
-        c.start()
 
     for c in pair:
         c.wait_recv()
@@ -365,6 +371,8 @@
         c.start()
 
     ng_ys = along_y(ng_at, ng_xs, ng_x, ng_t, ng_y, ny_s, ny_r)
+    for c in part_xs.values():
+        c.start()
     total = at_home(ng_at, ng_xs, ng_x, ng_ys, ng_y)
     m = mixed[...]
     centred = m - jnp.mean(m, axis=-1, keepdims=True)
@@ -580,12 +588,13 @@
             jax.ShapeDtypeStruct((NC, 2, NZ, w, HID), BF16),
             jax.ShapeDtypeStruct((NC, NZ, h, D), BF16),
         ),
-        in_specs=[vm] * 6
-        + [pl.BlockSpec(memory_space=pltpu.SMEM), vm]
-        + [pl.BlockSpec(memory_space=pl.ANY)] * 3,
+        in_specs=[vm, pl.BlockSpec(memory_space=pltpu.SMEM)]
+        + [pl.BlockSpec(memory_space=pltpu.HBM)] * 9,
         out_specs=[vm] * 5,
         scratch_shapes=[
-            v((D, HID), BF16), v((HID, D), BF16), v((SLOTS, D), BF16), v((SLOT_PAD, D), F32),
+            v((SLOTS, D), BF16), v((49, D), F32), v((D,), F32), v((D,), F32), v((HID,), F32),
+            v((D,), F32), v((HID, D), BF16), v((D, HID), BF16), v((SLOTS, D), BF16),
+            v((SLOT_PAD, D), F32),
             v(map_, BF16), v(map_, F32), v((PIX * 16, LANE), F32), v((49 * 16, LANE), F32),
             v((32, D), F32), v((PIX, D), F32),
             v((N_COL, PIX, D), BF16), v((band, D), BF16), v((every, D), BF16),
@@ -605,7 +614,7 @@
             v((NC, 16, 2, SUB, LANE), BF16), v((16, 2, SUB, LANE), BF16),
             v((16, 2, SUB, LANE), BF16), v((15, 2, SUB, LANE), BF16),
             v((2, SUB, LANE), BF16), v((16, 2, SUB, LANE), BF16), v((NC, 16, 2, SUB, LANE), BF16),
-            dma((3,)), dma((8,)), dma((8,)),
+            dma((9,)), dma((8,)), dma((8,)),
             dma((NY, NX)), dma((NY, NX)), dma((NY, NX)), dma((NY, NX)),
             dma((NX, NY)), dma((NX, NY)), dma((3,)), dma((3,)),
             dma((NX, NY)), dma((NX, NY)), dma((3,)), dma((3,)),
@@ -628,7 +637,7 @@
 ):
     feat = features.reshape(ROWS, COLS, SUB, LANE)
     seq, gin, gker, gup, gdown = whole(
-        feat, kernel, ln_gain, ln_bias, b_up, layer_scale, slot_token, seq_grad, w_up, w_down,
+        feat, slot_token, seq_grad, kernel, ln_gain, ln_bias, b_up, layer_scale, w_down, w_up,
         text_embed,
     )
     return (

time: 118 us -> 115 us (0.975)
  local copies, waits for them, and re-layouts: 10.8 us -> 8.49 us
    unnamed x24 -> x20, local copies, waits for them, and re-layouts: 8.99 us -> 6.72 us
where the time goes in v4:
time: 115 us; the launch traced here: 114 us
  Pallas kernels  105 us (91%)
  local copies, waits for them, and re-layouts  8.49 us (7%)
    pallas_call x1, Pallas kernels, whole(): pl.pallas_call(whole_kernel, out_shape=(jax.ShapeDtypeStruct((SLOTS, D),...  105 us
    unnamed x20, local copies, waits for them, and re-layouts  6.72 us

profile of v4, /device:TPU:1, one launch (start us, length us, event | category | flops | bytes accessed | tf_op | source)
XLA Modules:
  0.0 114.3 jit_solution(492449433852940318)
XLA Ops:
  0.6 0.0 copy-start
  0.6 1.0 reshape.22
  1.6 0.0 copy-start.3
  1.6 0.0 copy-start.4
  1.7 0.0 copy-start.5
  1.7 0.0 copy-done
  1.7 0.6 copy-done.3
  2.3 0.0 copy-done.4
  2.3 0.0 copy-done.5
  2.4 0.0 copy-start.1
  2.4 0.8 copy-done.1
  3.2 0.0 copy-start.2
  3.2 0.8 copy-done.2
  4.0 0.0 copy-start.6
  4.0 0.7 copy-done.6
  4.6 0.0 copy-start.7
  4.6 0.7 copy-done.7
  5.3 105.2 %shard_map.146 = (bf16[12,1536]{1,0:T(8,128)(2,1)S(1)}, bf16[4,6,12,128]{3,2,1,0:T(8,128)(2,1)S(1)}, f32[49,1536]{1,0:T(8,128)S(1)}, bf16[2,2,8,48,256]{4,3,2,1,0:T(8,128)(2,1)S(1)}, bf16[2,8,16,1536]{3,2,1,0:T(8,128)(2,1)S(1)}) custom-call(bf16[4,6,12,128]{3,2,1,0:T(8,128)(2,1)S(1)} %copy.18.feat, s32[12]{0:T(128)S(1)} %copy-done.7, ...), custom_call_target="tpu_custom_call" | custom-call | tf_op jit(solution)/shard_map/pallas_call | solution.py:582
  110.5 0.1 reshape.26
  110.6 0.7 copy.20
  111.2 0.6 copy.25
  111.9 0.7 copy.26
  112.6 0.9 copy.27
  113.5 0.9 copy.28
  (1 shorter events, 0.0 us)
Async XLA Ops:
  0.6 1.1 copy-start
  1.6 0.7 copy-start.3
  1.6 0.7 copy-start.4
  1.7 0.7 copy-start.5
  2.4 0.8 copy-start.1
  3.2 0.8 copy-start.2
  4.0 0.7 copy-start.6
  4.6 0.7 copy-start.7

commit v5 on v4

--- a/solution.py
+++ b/solution.py
@@ -456,6 +456,22 @@
     for c in k2:
         c.start()
 
+    def up_home(k):
+        return lax.rem(z - k + NZ, NZ)
+
+    down_far.wait_recv()
+    gdown[core, z] = (down_c[...].astype(F32) + down2[...].astype(F32)).astype(BF16)
+
+    def down_to(where, cc, zz, send, recv):
+        ref = gdown.at[cc, zz]
+        return remote(ref, ref, send, recv, where)
+
+    da = [down_to(zp[k], core, z, da_s.at[k], da_r.at[k]) for k in range(NZ - 1)]
+    dt = [down_to(twin, core, up_home(k), dt_s.at[k], dt_r.at[k]) for k in range(NZ)]
+    for c in da:
+        c.start()
+    dt[0].start()
+
     for c in halo:
         c.wait_recv()
     widen(mgpad, wide, row, col)
@@ -482,9 +498,6 @@
         ref = gup.at[cc, hh, zz]
         return remote(ref, ref, send, recv, where)
 
-    def up_home(k):
-        return lax.rem(z - k + NZ, NZ)
-
     ua = [up_to(zp[k], core, yh, z, ua_s.at[k], ua_r.at[k]) for k in range(NZ - 1)]
     uf = [up_to(far, core, yh, up_home(k), uf_s.at[k], uf_r.at[k]) for k in range(NZ)]
     ut = [up_to(twin, core, yh, up_home(k), ut_s.at[0, k], ut_r.at[0, k]) for k in range(NZ)]
@@ -493,19 +506,6 @@
         c.start()
     uf[0].start()
     ut[0].start()
-    down_far.wait_recv()
-    gdown[core, z] = (down_c[...].astype(F32) + down2[...].astype(F32)).astype(BF16)
-
-    def down_to(where, cc, zz, send, recv):
-        ref = gdown.at[cc, zz]
-        return remote(ref, ref, send, recv, where)
-
-    da = [down_to(zp[k], core, z, da_s.at[k], da_r.at[k]) for k in range(NZ - 1)]
-    dt = [down_to(twin, core, up_home(k), dt_s.at[k], dt_r.at[k]) for k in range(NZ)]
-    for c in da:
-        c.start()
-    dt[0].start()
-
     for k in range(15):
         k2[k].wait_recv()
     v = ker_z_in[0].astype(F32)
@@ -528,7 +528,7 @@
         live[:SLOTS] > 0.5, tok[:SLOTS].astype(BF16).astype(F32), text[...].astype(F32)
     ).astype(BF16)
 
-    for k in range(1, NZ):
+    for k in (1, 7, 2, 6, 3, 5, 4):
         b = up_home(k)
         up_to(zp[k - 1], core, yh, b, ua_s.at[k - 1], ua_r.at[k - 1]).wait_recv()
         uf[k].start()
@@ -548,7 +548,7 @@
         kflat[pl.ds(t * 16, SUB)] = ker_out[t % 2, t // 4, t // 2 % 2].astype(F32)
     for g in range(SUB):
         gker[:, g * LANE : (g + 1) * LANE] = kflat[pl.ds(g, 49, stride=16)]
-    for k in range(NZ):
+    for k in (0, 1, 7, 2, 6, 3, 5, 4):
         up_to(far, core, 1 - yh, up_home(k), uf_s.at[k], uf_r.at[k]).wait_recv()
         vt[k].start()
     for k in range(NZ):

time: 115 us -> 122 us (1.061)
  the two profiles are of different devices: /device:TPU:1 before, /device:TPU:15 now
where the time goes in v5:
time: 122 us; the launch traced here: 121 us
  Pallas kernels  112 us (92%)
  local copies, waits for them, and re-layouts  8.49 us (7%)
    pallas_call x1, Pallas kernels, whole(): pl.pallas_call(whole_kernel, out_shape=(jax.ShapeDtypeStruct((SLOTS, D),...  112 us
    unnamed x20, local copies, waits for them, and re-layouts  6.72 us

profile of v5, /device:TPU:15, one launch (start us, length us, event | category | flops | bytes accessed | tf_op | source)
XLA Modules:
  0.0 121.2 jit_solution(6745426879493547784)
XLA Ops:
  0.6 0.0 copy-start
  0.6 1.0 reshape.22
  1.6 0.0 copy-start.3
  1.6 0.0 copy-start.4
  1.7 0.0 copy-start.5
  1.7 0.0 copy-done
  1.7 0.6 copy-done.3
  2.3 0.0 copy-done.4
  2.3 0.0 copy-done.5
  2.4 0.0 copy-start.1
  2.4 0.8 copy-done.1
  3.2 0.0 copy-start.2
  3.2 0.8 copy-done.2
  4.0 0.0 copy-start.6
  4.0 0.7 copy-done.6
  4.6 0.0 copy-start.7
  4.6 0.7 copy-done.7
  5.3 112.0 %shard_map.146 = (bf16[12,1536]{1,0:T(8,128)(2,1)S(1)}, bf16[4,6,12,128]{3,2,1,0:T(8,128)(2,1)S(1)}, f32[49,1536]{1,0:T(8,128)S(1)}, bf16[2,2,8,48,256]{4,3,2,1,0:T(8,128)(2,1)S(1)}, bf16[2,8,16,1536]{3,2,1,0:T(8,128)(2,1)S(1)}) custom-call(bf16[4,6,12,128]{3,2,1,0:T(8,128)(2,1)S(1)} %copy.18.feat, s32[12]{0:T(128)S(1)} %copy-done.7, ...), custom_call_target="tpu_custom_call" | custom-call | tf_op jit(solution)/shard_map/pallas_call | solution.py:582
  117.3 0.1 reshape.26
  117.4 0.7 copy.20
  118.1 0.6 copy.25
  118.7 0.7 copy.26
  119.4 0.9 copy.27
  120.3 0.9 copy.28
  (1 shorter events, 0.0 us)
Async XLA Ops:
  0.6 1.1 copy-start
  1.6 0.7 copy-start.3
  1.6 0.7 copy-start.4
  1.7 0.7 copy-start.5
  2.4 0.8 copy-start.1
  3.2 0.8 copy-start.2
  4.0 0.7 copy-start.6
  4.6 0.7 copy-start.7
